TPU v7x, 512 devices: a whole 4x8x8 slice. The times are simulated.
512 devices in a mesh: rep: 8 (over y_hi, x), shard: 64 (over z, y_lo, core).
Axes of the slice: x: 4, y: 8 (y_hi: 2, y_lo: 4; y = y_hi * 4 + y_lo), z: 8, core: 2. Of those that a mesh axis runs over, the one named last changes fastest.
Arguments:
- hidden: bfloat16 [196608, 768], P(('rep', 'shard')), may hold values from -24 to 24
- prob: float32 [196608], P(('rep', 'shard')), may hold values from 0.05 to 0.5
- counts: int32 [512], P(('rep', 'shard')), may hold values from 96 to 384, as said below
- down_weight: bfloat16 [768, 2048], P('shard'), may hold values from -0.21875 to 0.21875
- cotangent: bfloat16 [196608, 2048], P(('rep', 'shard')), may hold values from -0.59765625 to 0.59765625
Outputs:
- output: bfloat16 [196608, 2048], P(('rep', 'shard'))
- grad_hidden: bfloat16 [196608, 768], P(('rep', 'shard'))
- grad_prob: float32 [196608], P(('rep', 'shard'))
- grad_weight: float32 [768, 2048], P('shard')
Inputs may be any that keep to these rules, and one draw needn't show every extreme that they name: Entry b counts the live rows at the start of block b of 384 slots; the rest of the block is padding; some block is full in every draw.
All inputs are finite; a program needn't handle non-finite values.
Results may differ from a plain program's by a relative error of at most 0.014.
Values may be sent and summed in bfloat16 or wider, within the bound.
A program may use at most 64 MiB of HBM per device.

v0:
```python
import jax
import jax.numpy as jnp
from jax import lax
from jax.sharding import PartitionSpec as P


def body(hidden, prob, counts, down_weight, cotangent):
    slots = hidden.shape[0]
    live = (jnp.arange(slots, dtype=jnp.int32) < counts[0]).astype(jnp.float32)
    weight = prob * live
    scaled = (weight[:, None] * cotangent.astype(jnp.float32)).astype(jnp.bfloat16)
    fore_weight = lax.all_gather(down_weight, "shard", axis=0, tiled=True)
    proj = jnp.dot(hidden, fore_weight, preferred_element_type=jnp.float32)
    back_weight = lax.all_gather(down_weight, "shard", axis=0, tiled=True)
    grad_hidden = lax.dot_general(
        scaled, back_weight, (((1,), (1,)), ((), ())), preferred_element_type=jnp.float32
    ).astype(jnp.bfloat16)
    output = (weight[:, None] * proj).astype(jnp.bfloat16)
    grad_prob = live * jnp.sum(cotangent.astype(jnp.float32) * proj, axis=1)
    partial_sum = lax.dot_general(
        hidden, scaled, (((0,), (0,)), ((), ())), preferred_element_type=jnp.float32
    ).astype(jnp.bfloat16)
    copy_sum = lax.psum_scatter(
        partial_sum.astype(jnp.float32).astype(jnp.bfloat16), "rep", scatter_dimension=1, tiled=True
    ).astype(jnp.float32)
    shard_sum = lax.psum_scatter(copy_sum, "shard", scatter_dimension=0, tiled=True)
    grad_weight = lax.all_gather(shard_sum, "rep", axis=1, tiled=True)
    return (output, grad_hidden, grad_prob, grad_weight)


def solution(mesh):
    placed = (
        P(("rep", "shard"), None),
        P(("rep", "shard")),
        P(("rep", "shard")),
        P("shard", None),
        P(("rep", "shard"), None),
    )
    return jax.shard_map(
        body,
        mesh=mesh,
        in_specs=placed,
        out_specs=(
            P(("rep", "shard"), None),
            P(("rep", "shard"), None),
            P(("rep", "shard")),
            P("shard", None),
        ),
        check_vma=False,
    )
```

profile of v0, /device:TPU:6, one launch (start us, length us, event | category | flops | bytes accessed | tf_op | source)
XLA Modules:
  0.0 502.5 jit_solution(11517149981112724678)
XLA Ops:
  8.0 0.0 copy-start
  8.0 0.0 all-gather.3.cloned.1.call-start
  8.1 0.7 all-gather.3.cloned.1.call-update
  8.7 0.0 reduce-scatter.3.cloned.1.call-start
  9.4 0.7 fusion.6
  10.1 0.0 copy-done
  10.1 5.0 %fusion.2 = bf16[768,2048]{0,1:T(8,128)(2,1)} fusion(bf16[384,768]{1,0:T(8,128)(2,1)S(1)} %copy-done, bf16[384,2048]{1,0:T(8,128)(2,1)} %param.9, f32[384]{0:T(512)S(1)} %fusion.6), kind=kOutput, calls=%fused_computation.6 | convolution fusion | flops 1211891712 | bytes 5309952 | tf_op jit(solution)/shard_map/dot_general | solution.py:20
  15.2 0.0 reduce-scatter.3.cloned.1.call-update
  15.2 1.3 dynamic-slice
  17.1 0.0 copy-start.2
  17.1 140.0 %all-gather.3.cloned.1.call-done = bf16[64,12,2048]{2,1,0:T(8,128)(2,1)} async-done(((bf16[1,12,2048]{2,1,0:T(8,128)(2,1)}), bf16[64,12,2048]{2,1,0:T(8,128)(2,1)}) %all-gather.3.cloned.1.call-update) | async-done | bytes 3145744 | tf_op jit(solution)/shard_map/all_gather | solution.py:12
  157.1 6.1 %reshape.10 = bf16[768,2048]{1,0:T(8,128)(2,1)} reshape(bf16[64,12,2048]{2,1,0:T(8,128)(2,1)} %all-gather.3.cloned.1.call-done) | data formatting | bytes 6291456
  163.2 0.0 copy-done.2
  163.2 0.0 copy-start.1
  163.2 4.7 fusion.1
  168.0 0.6 fusion.5
  168.5 0.0 copy-done.1
  168.5 2.3 convolution_convert_fusion.1
  170.8 0.0 reduce-scatter.3.cloned.1.call-done
  170.8 273.1 %all-reduce.2 = f32[768,256]{0,1:T(8,128)S(1)} all-reduce(bf16[768,256]{0,1:T(8,128)(2,1)} %reduce-scatter.3.cloned.1.call-done), channel_id=3, replica_groups=mesh['rep'=8,'shard'=64] {'shard'}, use_global_device_ids=true, to_apply=%region_2.0.clone | all-reduce | flops 196608 | bytes 1179648
  443.9 0.1 constant_dynamic-slice_fusion
  444.0 50.1 %all_gather.8 = f32[12,2048]{0,1:T(8,128)S(1)} all-gather(f32[12,256]{0,1:T(8,128)S(1)} %constant_dynamic-slice_fusion), channel_id=1, replica_groups=mesh['rep'=8,'shard'=64] {'rep'}, dimensions={1}, use_global_device_ids=true | all-gather | bytes 110592 | tf_op jit(solution)/shard_map/all_gather | solution.py:27
  494.1 1.0 copy.11
Async XLA Ops:
  8.0 2.1 copy-start
  8.0 149.1 %all-gather.3.cloned.1.call-start = ((), (), s32[]{:S(2)}) async-start(), calls=%async_computation.2 | async-start | bytes 4259840 | tf_op jit(solution)/shard_map/all_gather | solution.py:12
  8.7 162.1 %reduce-scatter.3.cloned.1.call-start = ((), (), s32[]{:S(2)}) async-start(), calls=%async_computation.1 | async-start | bytes 3538944 | tf_op jit(solution)/shard_map/reduce_scatter | solution.py:23
  17.1 146.1 %copy-start.2 = (bf16[384,2048]{1,0:T(8,128)(2,1)S(1)}, bf16[384,2048]{1,0:T(8,128)(2,1)}, u32[]{:S(2)}) copy-start(bf16[384,2048]{1,0:T(8,128)(2,1)} %param.9) | copy-start | bytes 4718596
  163.2 5.3 %copy-start.1 = (bf16[768,2048]{1,0:T(8,128)(2,1)S(1)}, bf16[768,2048]{1,0:T(8,128)(2,1)}, u32[]{:S(2)}) copy-start(bf16[768,2048]{1,0:T(8,128)(2,1)} %reshape.10) | copy-start | bytes 9437188
Sparse Core Ops, SparseCore 0:
  11.0 146.0 all-gather.2
Sparse Core Ops, SparseCore 1:
  15.3 119.8 reduce-scatter.2
where the time goes:
time: 503 us
  blocking collectives  323 us (64%)
  waiting for transfers between devices  141 us (28%)
  between operations  16.8 us (3%)
  matrix products  12 us (2%)
  local copies, waits for them, and re-layouts  8.52 us (2%)
    unnamed x1, blocking collectives  273 us
    all_gather x1, waiting for transfers between devices, body(): fore_weight = lax.all_gather(down_weight, 'shard', axis=0, tiled=True)  140 us
    all_gather x1, blocking collectives, body(): grad_weight = lax.all_gather(shard_sum, 'rep', axis=1, tiled=True)  50.1 us
  transfers between devices with their start and end apart: 2, of which 1 were waited for; matrix products, arithmetic and copies ran while one was open for 4% of the time, Pallas kernels for 0%

commit v1 on v0

v1 whole, which is shorter than its diff:
```python
import jax
import jax.numpy as jnp
from jax import lax
from jax.experimental import pallas as pl
from jax.experimental.pallas import tpu as pltpu
from jax.sharding import PartitionSpec as P

MESH = pl.DeviceIdType.MESH
F32, BF16 = jnp.float32, jnp.bfloat16
NX, NY, NZ, LO = 4, 8, 8, 4
ROWS, FF, D, SHARD = 384, 768, 2048, 12
SEMS = 144


def device(x, y, z, c):
    x, y, z, c = lax.rem(x, NX), lax.rem(y, NY), lax.rem(z, NZ), lax.rem(c, 2)
    return (lax.div(y, LO) * NX + x, z * (2 * LO) + lax.rem(y, LO) * 2 + c)


def kernel(
    hidden_h, prob_h, counts_s, weight_h, cot_h, out_h, gh_h, gp_h, gw_h,
    hid, hid_t, cot, scaled, prob, wgt, own_p, oth_p, rcv_p, ring, shard_in, shard, unit,
    blocks, full, out, gh_acc, gh, gp_acc, gp, send_z, recv_z, send_y, recv_y, recv_x, core_s, core_r, gw,
    local, ssem, rsem,
):
    r, s = lax.axis_index("rep"), lax.axis_index("shard")
    x, yh = lax.rem(r, NX), lax.div(r, NX)
    z, yl, c = lax.div(s, 2 * LO), lax.rem(lax.div(s, 2), LO), lax.rem(s, 2)
    y = yh * LO + yl
    px = lax.rem(x, 2)
    first = c == 0

    def at(dx=0, dy=0, dz=0, dc=0):
        return device(x + dx + NX, y + dy + NY, z + dz + NZ, c + dc)

    barrier = pltpu.get_barrier_semaphore()
    peers = [at(dc=1)] + [at(dx=k) for k in (1, 2, 3)]
    peers += [at(dy=k) for k in range(1, 8)] + [at(dz=k) for k in range(1, 8)]
    peers += [at(dy=4, dz=k) for k in range(1, 8)]
    for peer in peers:
        pl.semaphore_signal(barrier, inc=1, device_id=peer, device_id_type=MESH)

    loads = [
        pltpu.make_async_copy(a, b, local.at[i])
        for i, (a, b) in enumerate([(prob_h, prob), (hidden_h, hid), (cot_h, cot), (weight_h, shard_in)])
    ]
    for load in loads:
        load.start()

    used, sent = [0], []

    def group(n):
        used[0] += n
        assert used[0] <= SEMS
        return used[0] - n

    def push(src, dst, ssem_i, rsem_i, to):
        copy = pltpu.make_async_remote_copy(
            src, dst, ssem.at[ssem_i], rsem.at[rsem_i], device_id=to, device_id_type=MESH
        )
        copy.start()
        sent.append(copy)

    def arrive(dst, rsem_i):
        pltpu.make_async_remote_copy(
            dst, dst, ssem.at[0], rsem.at[rsem_i], device_id=at(dc=1), device_id_type=MESH
        ).wait_recv()

    loads[0].wait()
    place = lax.broadcasted_iota(jnp.int32, (1, ROWS), 1)
    live_row = (place < counts_s[0]).astype(F32)
    row = prob[...] * live_row
    wgt[...] = jnp.broadcast_to(row, (128, ROWS)).T
    loads[1].wait()
    hid_t[...] = hid[...].T
    loads[2].wait()
    for k in range(D // 128):
        at_k = pl.ds(128 * k, 128)
        scaled[:, at_k] = (wgt[...] * cot[:, at_k].astype(F32)).astype(BF16)
    loads[3].wait()
    shard[0] = jnp.concatenate([shard_in[...].astype(F32), jnp.zeros((4, D), F32)], axis=0).astype(BF16)

    for half, keep in ((1 - c, oth_p), (c, own_p)):
        for n in range(4):
            cols = pl.ds(pl.multiple_of(half * (D // 2) + 256 * n, 256), 256)
            part = jnp.dot(hid_t[...], scaled[:, cols], preferred_element_type=F32)
            if n < 2:
                keep[0, :, pl.ds(96 * n, 96), :] = part.astype(BF16).reshape(8, 96, 256)
            else:
                split = part.reshape(8, 4, 24, 256)
                for k in range(4):
                    keep[1, 4 * (n - 2) + k] = split[:, k].reshape(192, 256).astype(BF16)

    pl.semaphore_wait(barrier, len(peers))

    g_shard = group(1)
    push(shard.at[0], shard.at[1], g_shard, g_shard, at(dc=1))
    place_of = (z, y)
    order = [4, 3, -3, 2, -2, 1, -1, 0]
    g_pair = group(16)
    for i, k in enumerate(order):
        for a in range(2):
            dest = lax.rem(place_of[a] + k + 8, 8)
            push(oth_p.at[a, dest], rcv_p.at[a, dest], g_pair + 2 * i + a, g_pair + 2 * i + a, at(dc=1))

    paired = set()

    def pair(a, k):
        i = order.index(k)
        dest = lax.rem(place_of[a] + k + 8, 8)
        if (a, k) not in paired:
            paired.add((a, k))
            arrive(rcv_p.at[a, dest], g_pair + 2 * i + a)
        return dest

    g_ring = group(32)

    def slot(a, d, sub, t):
        return ((a * 2 + d) * 2 + sub) * 4 + t - 1

    def ring_step(t):
        for a in range(2):
            for d in range(2):
                for sub in ((0, 1) if d == 0 else (1, 0)):
                    if t == 1 and sub != d:
                        continue
                    k = (5 - t) * (1 if d == 0 else -1)
                    dest = pair(a, 4 if k == -4 else k)
                    rows = pl.ds(96 * sub, 96)
                    total = own_p[a, dest, rows, :].astype(F32) + rcv_p[a, dest, rows, :].astype(F32)
                    if t > 2 or (t == 2 and sub == d):
                        m = slot(a, d, sub, t - 1)
                        arrive(ring.at[m], g_ring + m)
                        total = total + ring[m].astype(F32)
                    own_p[a, dest, rows, :] = total.astype(BF16)
                    m = slot(a, d, sub, t)
                    step = 1 if d == 0 else -1
                    push(own_p.at[a, dest, rows, :], ring.at[m], g_ring + m, g_ring + m,
                         at(dz=step) if a == 0 else at(dy=step))

    def ring_end(a):
        dest = pair(a, 0)
        ends = []
        for sub in range(2):
            rows = pl.ds(96 * sub, 96)
            total = own_p[a, dest, rows, :].astype(F32) + rcv_p[a, dest, rows, :].astype(F32)
            for d in range(2):
                m = slot(a, d, sub, 4)
                arrive(ring.at[m], g_ring + m)
                total = total + ring[m].astype(F32)
            ends.append(total)
        return ends

    ring_step(1)

    q = c * 2 + px
    arrive(shard.at[1], g_shard)
    cols = pl.ds(pl.multiple_of(q * 512, 512), 512)
    mine, others = shard[0, :, cols].astype(F32)[:SHARD], shard[1, :, cols].astype(F32)[:SHARD]
    unit[0:SHARD, :] = jnp.where(first, mine, others)
    unit[SHARD : 2 * SHARD, :] = jnp.where(first, others, mine)
    u = unit[...]
    blocks[q, yl, z] = jnp.concatenate([u[:, :256], u[:, 256:]], axis=0).astype(BF16)
    g_wz = group(8)
    g_wz_s = group(7)
    for i, k in enumerate((4, 3, -3, 2, -2, 1, -1)):
        push(blocks.at[q, yl, z], blocks.at[q, yl, z], g_wz_s + i, g_wz + z, at(dz=k))

    ring_step(2)

    for k in range(1, 8):
        zk = lax.rem(z + k, 8)
        arrive(blocks.at[q, yl, zk], g_wz + zk)
    g_wy = group(4)
    low, high = pl.ds(0, 4), pl.ds(4, 4)
    push(blocks.at[q, yl], blocks.at[q, yl], g_wy, g_wy, at(dy=1))
    push(blocks.at[q, yl], blocks.at[q, yl], g_wy + 1, g_wy + 1, at(dy=-1))
    push(blocks.at[q, yl, low], blocks.at[q, yl, low], g_wy + 2, g_wy + 2, at(dy=2))
    push(blocks.at[q, yl, high], blocks.at[q, yl, high], g_wy + 3, g_wy + 3, at(dy=-2))

    g_wx, g_wc, g_wd = group(8), group(4), group(4)
    yls = [yl, lax.rem(yl + 3, 4), lax.rem(yl + 1, 4), lax.rem(yl + 2, 4)]

    def spread(j):
        ylj = yls[j]
        push(blocks.at[q, ylj, low], blocks.at[q, ylj, low], g_wx + j, g_wx + j, at(dx=1))
        push(blocks.at[q, ylj, high], blocks.at[q, ylj, high], g_wx + 4 + j, g_wx + 4 + j, at(dx=-1))
        push(blocks.at[q, ylj], blocks.at[q, ylj], g_wc + j, g_wc + j, at(dc=1))

    q2 = c * 2 + 1 - px

    def relay(j):
        ylj = yls[j]
        arrive(blocks.at[q2, ylj, low], g_wx + j)
        arrive(blocks.at[q2, ylj, high], g_wx + 4 + j)
        push(blocks.at[q2, ylj], blocks.at[q2, ylj], g_wd + j, g_wd + j, at(dc=1))

    spread(0)
    ring_step(3)
    ring_step(4)
    arrive(blocks.at[q, yls[1]], g_wy)
    spread(1)
    arrive(blocks.at[q, yls[2]], g_wy + 1)
    spread(2)

    ends = ring_end(0)
    for k in range(4):
        rows = slice(24 * k, 24 * k + 24)
        send_z[k] = jnp.concatenate([ends[0][rows], ends[1][rows]], axis=0).astype(BF16)
    g_z = group(8)
    g_z_s = group(7)
    for i, k in enumerate((4, 3, -3, 2, -2, 1, -1)):
        to = lax.rem(yl + k + 4, 4)
        push(send_z.at[to], recv_z.at[y], g_z_s + i, g_z + y, at(dy=k))
    recv_z[y] = send_z[yl]
    ends = ring_end(1)
    for k in range(8):
        block = ends[k // 4][24 * (k % 4) : 24 * (k % 4) + 24]
        send_y[k] = jnp.concatenate([block[:, :128], block[:, 128:]], axis=0).astype(BF16)
    g_y = group(16)
    g_y_s = group(15)
    me = yh * 8 + z
    for i, k in enumerate((4, 3, -3, 2, -2, 1, -1, 0)):
        to = lax.rem(z + k + 8, 8)
        push(send_y.at[to], recv_y.at[me], g_y_s + 2 * i, g_y + me, at(dy=4, dz=k))
        if k:
            push(send_y.at[to], recv_y.at[me], g_y_s + 2 * i + 1, g_y + me, at(dz=k))
    recv_y[me] = send_y[z]

    arrive(blocks.at[q, yls[3], low], g_wy + 2)
    arrive(blocks.at[q, yls[3], high], g_wy + 3)
    spread(3)

    def assemble(i, qi):
        for zi in range(8):
            for h in range(2):
                rows = [blocks[qi, k, zi, pl.ds(0, 48), :].astype(F32)[24 * h : 24 * h + 24] for k in range(4)]
                full[i, pl.ds(96 * zi, 96), pl.ds(256 * h, 256)] = jnp.concatenate(rows, axis=0).astype(BF16)

    stores = []

    def multiply(i, qi, start):
        cols = pl.ds(pl.multiple_of(qi * 512, 512), 512)
        proj = jnp.dot(hid[...], full[i], preferred_element_type=F32)
        for k in range(4):
            p = proj[:, 128 * k : 128 * k + 128]
            at_k = pl.ds(pl.multiple_of(qi * 512 + 128 * k, 128), 128)
            out[:, at_k] = (wgt[...] * p).astype(BF16)
            term = cot[:, at_k].astype(F32) * p
            gp_acc[...] = term if start and k == 0 else gp_acc[...] + term
        copy = pltpu.make_async_copy(out.at[:, cols], out_h.at[:, cols], local.at[4 + i])
        copy.start()
        stores.append(copy)
        back = lax.dot_general(scaled[:, cols], full[i], (((1,), (1,)), ((), ())), preferred_element_type=F32)
        gh_acc[...] = back if start else gh_acc[...] + back

    assemble(0, q)
    multiply(0, q, True)

    for k in range(1, 8):
        yk = lax.rem(y + k, 8)
        arrive(recv_z.at[yk], g_z + yk)
    total_z = recv_z[0].astype(F32)
    for k in range(1, 8):
        total_z = total_z + recv_z[k].astype(F32)
    for k in range(1, 16):
        mk = lax.rem(me + k, 16)
        arrive(recv_y.at[mk], g_y + mk)
    total_y = []
    for h in range(2):
        total = recv_y[8 * h].astype(F32)
        for k in range(1, 8):
            total = total + recv_y[8 * h + k].astype(F32)
        total_y.append(total)
    recv_x[x] = jnp.concatenate([total_z, jnp.concatenate(total_y, axis=1)], axis=0).astype(BF16)
    g_x = group(4)
    g_x_s = group(3)
    for i, k in enumerate((2, 1, 3)):
        push(recv_x.at[x], recv_x.at[x], g_x_s + i, g_x + x, at(dx=k))

    for j in range(3):
        relay(j)

    q3 = (1 - c) * 2 + px
    for j in range(4):
        arrive(blocks.at[q3, yls[j]], g_wc + j)
    assemble(1, q3)
    multiply(1, q3, False)
    relay(3)

    for k in range(1, 4):
        xk = lax.rem(x + k, 4)
        arrive(recv_x.at[xk], g_x + xk)
    total = recv_x[0].astype(F32)
    for k in range(1, 4):
        total = total + recv_x[k].astype(F32)
    core_s[...] = total
    g_core = group(1)
    push(core_s, core_r, g_core, g_core, at(dc=1))

    assemble(2, q2)
    multiply(2, q2, False)

    arrive(core_r, g_core)
    for h in range(2):
        f = jnp.where(first, core_s[...], core_r[...]) if h == 0 else jnp.where(first, core_r[...], core_s[...])
        parts = [f[0:24], f[24:48], f[48:72, :128], f[72:96, :128], f[48:72, 128:], f[72:96, 128:]]
        offset = h * (D // 2)
        for part in parts:
            width = part.shape[1]
            gw[:, pl.ds(offset, width)] = jnp.where(first, part[0:SHARD], part[SHARD:])
            offset += width
    copy = pltpu.make_async_copy(gw, gw_h, local.at[8])
    copy.start()
    stores.append(copy)

    q4 = (1 - c) * 2 + 1 - px
    for j in range(4):
        arrive(blocks.at[q4, yls[j]], g_wd + j)
    assemble(3, q4)
    multiply(3, q4, False)
    gh[...] = gh_acc[...].astype(BF16)
    copy = pltpu.make_async_copy(gh, gh_h, local.at[9])
    copy.start()
    stores.append(copy)
    gp[...] = live_row * jnp.sum(gp_acc[...].T, axis=0, keepdims=True)
    copy = pltpu.make_async_copy(gp, gp_h, local.at[10])
    copy.start()
    stores.append(copy)

    for copy in stores:
        copy.wait()
    for copy in sent:
        copy.wait_send()


def body(hidden, prob, counts, down_weight, cotangent):
    hbm = pl.BlockSpec(memory_space=pl.ANY)
    vmem = pltpu.VMEM
    output, grad_hidden, grad_prob, grad_weight = pl.pallas_call(
        kernel,
        name="expert_down",
        out_shape=(
            jax.ShapeDtypeStruct((ROWS, D), BF16),
            jax.ShapeDtypeStruct((ROWS, FF), BF16),
            jax.ShapeDtypeStruct((1, ROWS), F32),
            jax.ShapeDtypeStruct((SHARD, D), F32),
        ),
        in_specs=[hbm, hbm, pl.BlockSpec(memory_space=pltpu.SMEM), hbm, hbm],
        out_specs=(hbm, hbm, hbm, hbm),
        scratch_shapes=[
            vmem((ROWS, FF), BF16),
            vmem((FF, ROWS), BF16),
            vmem((ROWS, D), BF16),
            vmem((ROWS, D), BF16),
            vmem((1, ROWS), F32),
            vmem((ROWS, 128), F32),
            vmem((2, 8, 192, 256), BF16),
            vmem((2, 8, 192, 256), BF16),
            vmem((2, 8, 192, 256), BF16),
            vmem((32, 96, 256), BF16),
            vmem((SHARD, D), BF16),
            vmem((2, 16, D), BF16),
            vmem((2 * SHARD, 512), F32),
            vmem((4, 4, 8, 48, 256), BF16),
            vmem((4, FF, 512), BF16),
            vmem((ROWS, D), BF16),
            vmem((ROWS, FF), F32),
            vmem((ROWS, FF), BF16),
            vmem((ROWS, 128), F32),
            vmem((1, ROWS), F32),
            vmem((4, 48, 256), BF16),
            vmem((8, 48, 256), BF16),
            vmem((8, 48, 128), BF16),
            vmem((16, 48, 128), BF16),
            vmem((4, 96, 256), BF16),
            vmem((96, 256), F32),
            vmem((96, 256), F32),
            vmem((SHARD, D), F32),
            pltpu.SemaphoreType.DMA((11,)),
            pltpu.SemaphoreType.DMA((SEMS,)),
            pltpu.SemaphoreType.DMA((SEMS,)),
        ],
        compiler_params=pltpu.CompilerParams(
            collective_id=0, has_side_effects=True, vmem_limit_bytes=48 * 2**20
        ),
    )(hidden, prob.reshape(1, ROWS), counts, down_weight, cotangent)
    return output, grad_hidden, grad_prob.reshape(ROWS), grad_weight


def solution(mesh):
    placed = (
        P(("rep", "shard"), None),
        P(("rep", "shard")),
        P(("rep", "shard")),
        P("shard", None),
        P(("rep", "shard"), None),
    )
    return jax.shard_map(
        body,
        mesh=mesh,
        in_specs=placed,
        out_specs=(
            P(("rep", "shard"), None),
            P(("rep", "shard"), None),
            P(("rep", "shard")),
            P("shard", None),
        ),
        check_vma=False,
    )
```

time: 503 us -> 73.3 us (0.15)
  the two profiles are of different devices: /device:TPU:6 before, /device:TPU:57 now
where the time goes in v1:
time: 73.3 us; the launch traced here: 73.1 us
  Pallas kernels  64.6 us (88%)
  local copies, waits for them, and re-layouts  6.61 us (9%)
  between operations  1.29 us (2%)
    pallas_call x1, Pallas kernels, body(): pl.pallas_call(kernel, name='expert_down', out_shape=(jax.ShapeDtypeStruc...  64.6 us
    unnamed x9, local copies, waits for them, and re-layouts  5.92 us

profile of v1, /device:TPU:57, one launch (start us, length us, event | category | flops | bytes accessed | tf_op | source)
XLA Modules:
  0.0 73.1 jit_solution(8177297284845498905)
XLA Ops:
  1.3 0.7 reshape.14.prob_h
  2.0 0.0 copy-start
  2.0 1.4 %copy-done = bf16[384,2048]{1,0:T(8,128)(2,1)S(1)} copy-done((bf16[384,2048]{1,0:T(8,128)(2,1)S(1)}, bf16[384,2048]{1,0:T(8,128)(2,1)}, u32[]{:S(2)}) %copy-start) | copy-done | bytes 1572888
  3.4 0.0 copy-start.1
  3.4 1.1 %copy-done.1 = bf16[384,768]{1,0:T(8,128)(2,1)S(1)} copy-done((bf16[384,768]{1,0:T(8,128)(2,1)S(1)}, bf16[384,768]{1,0:T(8,128)(2,1)}, u32[]{:S(2)}) %copy-start.1) | copy-done | bytes 589848
  4.4 0.0 copy-start.2
  4.4 0.8 %copy-done.2 = bf16[12,2048]{1,0:T(8,128)(2,1)S(1)} copy-done((bf16[12,2048]{1,0:T(8,128)(2,1)S(1)}, bf16[12,2048]{1,0:T(8,128)(2,1)}, u32[]{:S(2)}) %copy-start.2) | copy-done | bytes 49176
  5.3 64.6 %expert_down.1 = (bf16[384,2048]{1,0:T(8,128)(2,1)S(1)}, bf16[384,768]{1,0:T(8,128)(2,1)S(1)}, f32[1,384]{1,0:T(1,128)S(1)}, f32[12,2048]{1,0:T(8,128)S(1)}) custom-call(bf16[384,768]{1,0:T(8,128)(2,1)S(1)} %copy-done.1, f32[1,384]{1,0:T(1,128)S(1)} %reshape.14.prob_h, s32[1]{0:T(128)S(6)} %copy.12.counts_s, bf16[12,2048]{1,0:T(8,128)(2,1)S(1)} %copy-done.2, ...), custom_call_target="tpu_custom_call" | custom-call | tf_op jit(solution)/shard_map/expert_down/pallas_call | solution.py:340
  69.9 0.6 reduce
  70.5 1.1 %copy.13 = bf16[384,2048]{1,0:T(8,128)(2,1)} copy(bf16[384,2048]{1,0:T(8,128)(2,1)S(1)} %get-tuple-element.16) | data formatting | bytes 3145728
  71.6 0.8 %copy.14 = bf16[384,768]{1,0:T(8,128)(2,1)} copy(bf16[384,768]{1,0:T(8,128)(2,1)S(1)} %get-tuple-element.17) | data formatting | bytes 1179648
  72.4 0.7 copy.15
Async XLA Ops:
  2.0 1.4 %copy-start = (bf16[384,2048]{1,0:T(8,128)(2,1)S(1)}, bf16[384,2048]{1,0:T(8,128)(2,1)}, u32[]{:S(2)}) copy-start(bf16[384,2048]{1,0:T(8,128)(2,1)} %cot_h.1) | copy-start | bytes 4718596
  3.4 1.1 %copy-start.1 = (bf16[384,768]{1,0:T(8,128)(2,1)S(1)}, bf16[384,768]{1,0:T(8,128)(2,1)}, u32[]{:S(2)}) copy-start(bf16[384,768]{1,0:T(8,128)(2,1)} %hidden_h.1) | copy-start | bytes 1769476
  4.4 0.8 %copy-start.2 = (bf16[12,2048]{1,0:T(8,128)(2,1)S(1)}, bf16[12,2048]{1,0:T(8,128)(2,1)}, u32[]{:S(2)}) copy-start(bf16[12,2048]{1,0:T(8,128)(2,1)} %weight_h.1) | copy-start | bytes 147460

commit v2 on v0

v2 whole, which is shorter than its diff:
```python
import jax
import jax.numpy as jnp
from jax import lax
from jax.experimental import pallas as pl
from jax.experimental.pallas import tpu as pltpu
from jax.sharding import PartitionSpec as P

AG, RS = True, True
MESH = pl.DeviceIdType.MESH
F32, BF16 = jnp.float32, jnp.bfloat16
NX, NY, NZ, LO = 4, 8, 8, 4
ROWS, FF, D, SHARD = 384, 768, 2048, 12
SEMS = 192


def device(x, y, z, c):
    x, y, z, c = lax.rem(x, NX), lax.rem(y, NY), lax.rem(z, NZ), lax.rem(c, 2)
    return (lax.div(y, LO) * NX + x, z * (2 * LO) + lax.rem(y, LO) * 2 + c)


def kernel(
    hidden_h, prob_h, counts_s, weight_h, cot_h, out_h, gh_h, gp_h, gw_h,
    hid, hid_t, cot, scaled, prob, wgt, own_z, own_x, oth_z, oth_x, rcv_z, rcv_x, ring_z, ring_x, shard_in, shard, unit,
    blocks, full, out, gh_acc, gh, gp_acc, gp, send_z, recv_z, send_yz, recv_yz, send_yx, recv_yx, recv_x, core_s, core_r, gw,
    local, ssem, rsem,
):
    r, s = lax.axis_index("rep"), lax.axis_index("shard")
    x, yh = lax.rem(r, NX), lax.div(r, NX)
    z, yl, c = lax.div(s, 2 * LO), lax.rem(lax.div(s, 2), LO), lax.rem(s, 2)
    y = yh * LO + yl
    first = c == 0

    def at(dx=0, dy=0, dz=0, dc=0):
        return device(x + dx + NX, y + dy + NY, z + dz + NZ, c + dc)

    barrier = pltpu.get_barrier_semaphore()
    peers = [at(dc=1)] + [at(dx=k) for k in (1, 2, 3)]
    peers += [at(dy=k) for k in range(1, 8)] + [at(dz=k) for k in range(1, 8)]
    for peer in peers:
        pl.semaphore_signal(barrier, inc=1, device_id=peer, device_id_type=MESH)

    loads = [
        pltpu.make_async_copy(a, b, local.at[i])
        for i, (a, b) in enumerate([(prob_h, prob), (hidden_h, hid), (weight_h, shard_in)])
    ]
    for load in loads:
        load.start()
    cot_loads = []
    for i, half in enumerate((1 - c, c)):
        cols = pl.ds(pl.multiple_of(half * (D // 2), D // 2), D // 2)
        load = pltpu.make_async_copy(cot_h.at[:, cols], cot.at[:, cols], local.at[3 + i])
        load.start()
        cot_loads.append(load)

    used, sent = [0], []

    def group(n):
        used[0] += n
        assert used[0] <= SEMS
        return used[0] - n

    def push(src, dst, ssem_i, rsem_i, to):
        copy = pltpu.make_async_remote_copy(
            src, dst, ssem.at[ssem_i], rsem.at[rsem_i], device_id=to, device_id_type=MESH
        )
        copy.start()
        sent.append(copy)

    def arrive(dst, rsem_i):
        pltpu.make_async_remote_copy(
            dst, dst, ssem.at[0], rsem.at[rsem_i], device_id=at(dc=1), device_id_type=MESH
        ).wait_recv()

    loads[0].wait()
    place = lax.broadcasted_iota(jnp.int32, (1, ROWS), 1)
    live_row = (place < counts_s[0]).astype(F32)
    row = prob[...].reshape(1, ROWS) * live_row
    wgt[...] = jnp.broadcast_to(row, (128, ROWS)).T
    loads[1].wait()
    hid_t[...] = hid[...].T

    def partials(half, keep_z, keep_x, ns):
        for n in ns:
            start = half * (D // 2) + 256 * n
            for k in range(2):
                at_k = pl.ds(pl.multiple_of(start + 128 * k, 128), 128)
                scaled[:, at_k] = (wgt[...] * cot[:, at_k].astype(F32)).astype(BF16)
            cols = pl.ds(pl.multiple_of(start, 256), 256)
            part = jnp.dot(hid_t[...], scaled[:, cols], preferred_element_type=F32)
            if n < 2:
                keep_z[:, pl.ds(96 * n, 96), :] = part.astype(BF16).reshape(8, 96, 256)
            else:
                for k in range(2):
                    keep_x[2 * (n - 2) + k] = part[:, 128 * k : 128 * k + 128].astype(BF16)

    orders = ([4, 3, -3, 2, -2, 1, -1, 0], [2, 1, -1, 0])
    place_of, length = (z, x), (NZ, NX)
    own, oth, rcv = (own_z, own_x), (oth_z, oth_x), (rcv_z, rcv_x)
    g_shard, g_pair = group(1), (group(8), group(4))

    def push_pair(a):
        for i, k in enumerate(orders[a] if RS else []):
            dest = lax.rem(place_of[a] + k + length[a], length[a])
            push(oth[a].at[dest], rcv[a].at[dest], g_pair[a] + i, g_pair[a] + i, at(dc=1))

    cot_loads[0].wait()
    partials(1 - c, oth_z, oth_x, (0, 1))
    loads[2].wait()
    shard[0] = jnp.concatenate([shard_in[...].astype(F32), jnp.zeros((4, D), F32)], axis=0).astype(BF16)
    def rs(f, *args):
        return f(*args) if RS else None

    def ag(f, *args):
        return f(*args) if AG else None

    qs = [c * 4 + lax.rem(x + k, 4) for k in range(4)] + [(1 - c) * 4 + lax.rem(x + k, 4) for k in range(4)]
    yls = [yl, lax.rem(yl + 3, 4), lax.rem(yl + 1, 4), lax.rem(yl + 2, 4)]
    low, high = pl.ds(0, 4), pl.ds(4, 4)
    g_wz, g_wz_s, g_wy, g_wx, g_wc = group(8), group(7), group(4), group(16), group(16)

    def make_unit():
        q = qs[0]
        arrive(shard.at[1], g_shard)
        cols = pl.ds(pl.multiple_of(q * 256, 256), 256)
        mine, others = shard[0, :, cols].astype(F32)[:SHARD], shard[1, :, cols].astype(F32)[:SHARD]
        unit[0:SHARD, :] = jnp.where(first, mine, others)
        unit[SHARD : 2 * SHARD, :] = jnp.where(first, others, mine)
        u = unit[...]
        blocks[q, yl, z] = jnp.concatenate([u[:, :128], u[:, 128:]], axis=0).astype(BF16)
        for i, k in enumerate((4, 3, -3, 2, -2, 1, -1)):
            push(blocks.at[q, yl, z], blocks.at[q, yl, z], g_wz_s + i, g_wz + z, at(dz=k))

    def along_y():
        q = qs[0]
        for k in range(1, 8):
            zk = lax.rem(z + k, 8)
            arrive(blocks.at[q, yl, zk], g_wz + zk)
        push(blocks.at[q, yl], blocks.at[q, yl], g_wy, g_wy, at(dy=1))
        push(blocks.at[q, yl], blocks.at[q, yl], g_wy + 1, g_wy + 1, at(dy=-1))
        push(blocks.at[q, yl, low], blocks.at[q, yl, low], g_wy + 2, g_wy + 2, at(dy=2))
        push(blocks.at[q, yl, high], blocks.at[q, yl, high], g_wy + 3, g_wy + 3, at(dy=-2))

    pl.semaphore_wait(barrier, len(peers))
    if AG:
        push(shard.at[0], shard.at[1], g_shard, g_shard, at(dc=1))
    push_pair(0)
    partials(1 - c, oth_z, oth_x, (2, 3))
    push_pair(1)
    if AG:
        make_unit()
    cot_loads[1].wait()
    partials(c, own_z, own_x, (0, 1, 2, 3))

    paired = set()

    def pair(a, k):
        k = length[a] // 2 if k == -length[a] // 2 else k
        dest = lax.rem(place_of[a] + k + length[a], length[a])
        if (a, k) not in paired:
            paired.add((a, k))
            arrive(rcv[a].at[dest], g_pair[a] + orders[a].index(k))
        return dest

    rings, height = (ring_z, ring_x), (48, 192)
    g_ring = (group(32), group(16))

    def slot(a, d, sub, t):
        return ((d * 4) + sub) * (length[a] // 2) + t - 1

    def ring_step(a, t):
        for i in range(2 if t == 1 else 4):
            for d in range(2):
                far = t == 1 or i >= 2
                sub = (i % 2) + 2 * (d if far else 1 - d)
                dest = pair(a, (length[a] // 2 + 1 - t) * (1 if d == 0 else -1))
                rows = pl.ds(height[a] * sub, height[a])
                total = own[a][dest, rows, :].astype(F32) + rcv[a][dest, rows, :].astype(F32)
                if t > 2 or (t == 2 and far):
                    m = slot(a, d, sub, t - 1)
                    arrive(rings[a].at[m], g_ring[a] + m)
                    total = total + rings[a][m].astype(F32)
                own[a][dest, rows, :] = total.astype(BF16)
                m = slot(a, d, sub, t)
                step = 1 if d == 0 else -1
                push(own[a].at[dest, rows, :], rings[a].at[m], g_ring[a] + m, g_ring[a] + m,
                     at(dz=step) if a == 0 else at(dx=step))

    def ring_end(a):
        dest = pair(a, 0)
        ends = []
        for sub in range(4):
            rows = pl.ds(height[a] * sub, height[a])
            ends.append(own[a][dest, rows, :].astype(F32) + rcv[a][dest, rows, :].astype(F32))
        for i in range(4):
            for d in range(2):
                sub = (i % 2) + 2 * (1 - d if i < 2 else d)
                m = slot(a, d, sub, length[a] // 2)
                arrive(rings[a].at[m], g_ring[a] + m)
                ends[sub] = ends[sub] + rings[a][m].astype(F32)
        return ends

    def to_core(k, j):
        block = blocks.at[qs[k], yls[j]]
        push(block, block, g_wc + 4 * k + j, g_wc + 4 * k + j, at(dc=1))

    def spread(j):
        if j in (1, 2):
            arrive(blocks.at[qs[0], yls[j]], g_wy + j - 1)
        if j == 3:
            arrive(blocks.at[qs[0], yls[3], low], g_wy + 2)
            arrive(blocks.at[qs[0], yls[3], high], g_wy + 3)
        block = blocks.at[qs[0], yls[j]]
        push(block, block, g_wx + j, g_wx + j, at(dx=1))
        push(block, block, g_wx + 4 + j, g_wx + 4 + j, at(dx=-1))
        to_core(0, j)

    def forward(j):
        arrive(blocks.at[qs[3], yls[j]], g_wx + j)
        part = blocks.at[qs[3], yls[j], low]
        push(part, part, g_wx + 8 + j, g_wx + 8 + j, at(dx=1))
        arrive(blocks.at[qs[1], yls[j]], g_wx + 4 + j)
        part = blocks.at[qs[1], yls[j], high]
        push(part, part, g_wx + 12 + j, g_wx + 12 + j, at(dx=-1))
        to_core(3, j)
        to_core(1, j)

    def last(j):
        arrive(blocks.at[qs[2], yls[j], low], g_wx + 8 + j)
        arrive(blocks.at[qs[2], yls[j], high], g_wx + 12 + j)
        to_core(2, j)

    stores = []

    def multiply(i):
        if i >= 4:
            for j in range(4):
                arrive(blocks.at[qs[i], yls[j]], g_wc + 4 * (i - 4) + j)
        qi = qs[i]
        for zi in range(8):
            for h in range(2):
                rows = [blocks[qi, k, zi].astype(F32)[24 * h : 24 * h + 24] for k in range(4)]
                full[i, pl.ds(96 * zi, 96), pl.ds(128 * h, 128)] = jnp.concatenate(rows, axis=0).astype(BF16)
        cols = pl.ds(pl.multiple_of(qi * 256, 256), 256)
        proj = jnp.dot(hid[...], full[i], preferred_element_type=F32)
        for k in range(2):
            p = proj[:, 128 * k : 128 * k + 128]
            at_k = pl.ds(pl.multiple_of(qi * 256 + 128 * k, 128), 128)
            out[:, at_k] = (wgt[...] * p).astype(BF16)
            term = cot[:, at_k].astype(F32) * p
            gp_acc[...] = term if not stores and k == 0 else gp_acc[...] + term
        back = lax.dot_general(scaled[:, cols], full[i], (((1,), (1,)), ((), ())), preferred_element_type=F32)
        gh_acc[...] = back if not stores else gh_acc[...] + back
        copy = pltpu.make_async_copy(out.at[:, cols], out_h.at[:, cols], local.at[5 + i])
        copy.start()
        stores.append(copy)

    far_first = (4, 3, -3, 2, -2, 1, -1)
    g_z, g_z_s, g_yz, g_yz_s, g_yx, g_yx_s = group(8), group(7), group(8), group(7), group(8), group(7)
    g_x, g_x_s, g_core = group(4), group(3), group(1)
    none = jnp.zeros((8, 128), F32)

    def across_z():
        ends = ring_end(1)
        for k in range(8):
            send_z[k] = ends[k // 2][96 * (k % 2) : 96 * (k % 2) + 96].astype(BF16)
        for i, k in enumerate(far_first):
            to = lax.rem(z + k + 8, 8)
            push(send_z.at[to], recv_z.at[z], g_z_s + i, g_z + z, at(dz=k))
        recv_z[z] = send_z[z]

    def across_y(send, recv, base, base_s):
        for i, k in enumerate(far_first):
            to = lax.rem(yl + k + 4, 4)
            push(send.at[to], recv.at[y], base_s + i, base + y, at(dy=k))
        recv[y] = send[yl]

    def across_y_z():
        ends = ring_end(0)
        for k in range(4):
            rows = slice(24 * (k % 2), 24 * (k % 2) + 24)
            low_cols, high_cols = ends[k // 2][rows], ends[2 + k // 2][rows]
            parts = [low_cols[:, :128], low_cols[:, 128:], high_cols[:, :128], high_cols[:, 128:]]
            send_yz[k] = jnp.concatenate(parts, axis=0).astype(BF16)
        across_y(send_yz, recv_yz, g_yz, g_yz_s)

    def gathered(recv, base, mine, n):
        for k in range(1, n):
            at_k = lax.rem(mine + k, n)
            arrive(recv.at[at_k], base + at_k)
        total = recv[0].astype(F32)
        for k in range(1, n):
            total = total + recv[k].astype(F32)
        return total

    def across_y_x():
        total = gathered(recv_z, g_z, z, 8)
        for k in range(4):
            send_yx[k] = jnp.concatenate([total[24 * k : 24 * k + 24], none], axis=0).astype(BF16)
        across_y(send_yx, recv_yx, g_yx, g_yx_s)

    def exchange_x():
        total_z = gathered(recv_yz, g_yz, y, 8)
        total_x = gathered(recv_yx, g_yx, y, 8)
        recv_x[x] = jnp.concatenate([total_z, total_x], axis=0).astype(BF16)
        for i, k in enumerate((2, 1, 3)):
            push(recv_x.at[x], recv_x.at[x], g_x_s + i, g_x + x, at(dx=k))

    def exchange_core():
        total = gathered(recv_x, g_x, x, 4)
        core_s[pl.ds(0, 96), :] = total[:96]
        for k in range(4):
            core_s[pl.ds(96 + 24 * k, 24), :] = recv_x[k].astype(F32)[96:120]
        push(core_s, core_r, g_core, g_core, at(dc=1))

    def finish_sum():
        arrive(core_r, g_core)
        for h in range(2):
            f = jnp.where(first, core_s[...], core_r[...]) if h == 0 else jnp.where(first, core_r[...], core_s[...])
            for k in range(8):
                part = f[24 * k : 24 * k + 24]
                gw[:, pl.ds(h * (D // 2) + 128 * k, 128)] = jnp.where(first, part[:SHARD], part[SHARD:])
        copy = pltpu.make_async_copy(gw, gw_h, local.at[13])
        copy.start()
        stores.append(copy)

    rs(ring_step, 0, 1)
    rs(ring_step, 1, 1)
    rs(ring_step, 1, 2)
    rs(ring_step, 0, 2)
    ag(along_y)
    ag(spread, 0)
    rs(ring_step, 0, 3)
    rs(ring_step, 0, 4)
    rs(across_z)
    ag(spread, 1)
    ag(spread, 2)
    ag(forward, 0)
    rs(across_y_z)
    ag(spread, 3)
    rs(across_y_x)
    ag(multiply, 0)
    ag(forward, 1)
    ag(forward, 2)
    ag(multiply, 4)
    rs(exchange_x)
    ag(forward, 3)
    for j in range(3):
        ag(last, j)
    ag(multiply, 1)
    ag(multiply, 3)
    rs(exchange_core)
    ag(last, 3)
    ag(multiply, 5)
    rs(finish_sum)
    ag(multiply, 7)
    ag(multiply, 2)
    ag(multiply, 6)
    gh[...] = gh_acc[...].astype(BF16)
    copy = pltpu.make_async_copy(gh, gh_h, local.at[13])
    copy.start()
    stores.append(copy)
    gp[...] = (live_row * jnp.sum(gp_acc[...].T, axis=0, keepdims=True)).reshape(ROWS)
    copy = pltpu.make_async_copy(gp, gp_h, local.at[14])
    copy.start()
    stores.append(copy)

    for copy in stores:
        copy.wait()
    for copy in sent:
        copy.wait_send()


def pin(a):
    return pltpu.with_memory_space_constraint(a, pltpu.HBM)


def body(hidden, prob, counts, down_weight, cotangent):
    hbm = pl.BlockSpec(memory_space=pltpu.HBM)
    free = pl.BlockSpec(memory_space=pl.ANY)
    vmem = pltpu.VMEM
    output, grad_hidden, grad_prob, grad_weight = pl.pallas_call(
        kernel,
        name="expert_down",
        out_shape=(
            jax.ShapeDtypeStruct((ROWS, D), BF16),
            jax.ShapeDtypeStruct((ROWS, FF), BF16),
            jax.ShapeDtypeStruct((ROWS,), F32),
            jax.ShapeDtypeStruct((SHARD, D), F32),
        ),
        in_specs=[hbm, hbm, pl.BlockSpec(memory_space=pltpu.SMEM), hbm, hbm],
        out_specs=(free, free, free, free),
        scratch_shapes=[
            vmem((ROWS, FF), BF16),
            vmem((FF, ROWS), BF16),
            vmem((ROWS, D), BF16),
            vmem((ROWS, D), BF16),
            vmem((ROWS,), F32),
            vmem((ROWS, 128), F32),
            vmem((8, 192, 256), BF16),
            vmem((4, FF, 128), BF16),
            vmem((8, 192, 256), BF16),
            vmem((4, FF, 128), BF16),
            vmem((8, 192, 256), BF16),
            vmem((4, FF, 128), BF16),
            vmem((32, 48, 256), BF16),
            vmem((16, 192, 128), BF16),
            vmem((SHARD, D), BF16),
            vmem((2, 16, D), BF16),
            vmem((2 * SHARD, 256), F32),
            vmem((8, 4, 8, 48, 128), BF16),
            vmem((8, FF, 256), BF16),
            vmem((ROWS, D), BF16),
            vmem((ROWS, FF), F32),
            vmem((ROWS, FF), BF16),
            vmem((ROWS, 128), F32),
            vmem((ROWS,), F32),
            vmem((8, 96, 128), BF16),
            vmem((8, 96, 128), BF16),
            vmem((4, 96, 128), BF16),
            vmem((8, 96, 128), BF16),
            vmem((4, 32, 128), BF16),
            vmem((8, 32, 128), BF16),
            vmem((4, 128, 128), BF16),
            vmem((192, 128), F32),
            vmem((192, 128), F32),
            vmem((SHARD, D), F32),
            pltpu.SemaphoreType.DMA((16,)),
            pltpu.SemaphoreType.DMA((SEMS,)),
            pltpu.SemaphoreType.DMA((SEMS,)),
        ],
        compiler_params=pltpu.CompilerParams(
            collective_id=0, has_side_effects=True, vmem_limit_bytes=40 * 2**20
        ),
    )(pin(hidden), pin(prob), counts, pin(down_weight), pin(cotangent))
    return output, grad_hidden, grad_prob, grad_weight


def solution(mesh):
    placed = (
        P(("rep", "shard"), None),
        P(("rep", "shard")),
        P(("rep", "shard")),
        P("shard", None),
        P(("rep", "shard"), None),
    )
    return jax.shard_map(
        body,
        mesh=mesh,
        in_specs=placed,
        out_specs=(
            P(("rep", "shard"), None),
            P(("rep", "shard"), None),
            P(("rep", "shard")),
            P("shard", None),
        ),
        check_vma=False,
    )
```

time: 503 us -> 58.4 us (0.12)
  the two profiles are of different devices: /device:TPU:6 before, /device:TPU:1 now
where the time goes in v2:
time: 58.4 us; the launch traced here: 58.2 us
  Pallas kernels  53.7 us (92%)
  local copies, waits for them, and re-layouts  3.19 us (5%)
  between operations  1.29 us (2%)
    pallas_call x1, Pallas kernels, body(): pl.pallas_call(kernel, name='expert_down', out_shape=(jax.ShapeDtypeStruc...  53.7 us
    unnamed x4, local copies, waits for them, and re-layouts  3.19 us

profile of v2, /device:TPU:1, one launch (start us, length us, event | category | flops | bytes accessed | tf_op | source)
XLA Modules:
  0.0 58.2 jit_solution(5847990159588538970)
XLA Ops:
  1.3 53.7 %expert_down.1 = (bf16[384,2048]{1,0:T(8,128)(2,1)S(1)}, bf16[384,768]{1,0:T(8,128)(2,1)S(1)}, f32[384]{0:T(512)S(1)}, f32[12,2048]{1,0:T(8,128)S(1)}) custom-call(bf16[384,768]{1,0:T(8,128)(2,1)} %hidden_h.1, f32[384]{0:T(512)} %prob_h.1, s32[1]{0:T(128)S(6)} %copy.13.counts_s, bf16[12,2048]{1,0:T(8,128)(2,1)} %weight_h.1, bf16[384,2048]{1,0:T(8,128)(2,1)} %cot_h.1), custom_call_target="tpu_custom_call" | custom-call | tf_op jit(solution)/shard_map/expert_down/pallas_call | solution.py:381
  55.0 1.1 %copy.14 = bf16[384,2048]{1,0:T(8,128)(2,1)} copy(bf16[384,2048]{1,0:T(8,128)(2,1)S(1)} %get-tuple-element.8) | data formatting | bytes 3145728
  56.2 0.8 %copy.15 = bf16[384,768]{1,0:T(8,128)(2,1)} copy(bf16[384,768]{1,0:T(8,128)(2,1)S(1)} %get-tuple-element.9) | data formatting | bytes 1179648
  57.0 0.6 copy.16
  57.6 0.7 %copy.17 = f32[12,2048]{1,0:T(8,128)} copy(f32[12,2048]{1,0:T(8,128)S(1)} %get-tuple-element.11) | data formatting | bytes 196608

commit v3 on v2

--- a/solution.py
+++ b/solution.py
@@ -5,12 +5,11 @@
 from jax.experimental.pallas import tpu as pltpu
 from jax.sharding import PartitionSpec as P
 
-AG, RS = True, True
 MESH = pl.DeviceIdType.MESH
 F32, BF16 = jnp.float32, jnp.bfloat16
 NX, NY, NZ, LO = 4, 8, 8, 4
 ROWS, FF, D, SHARD = 384, 768, 2048, 12
-SEMS = 192
+SEMS, KINDS = 78, 15
 
 
 def device(x, y, z, c):
@@ -52,19 +51,21 @@
         load.start()
         cot_loads.append(load)
 
-    used, sent = [0], []
+    used, sends = [0], []
 
     def group(n):
         used[0] += n
         assert used[0] <= SEMS
         return used[0] - n
 
-    def push(src, dst, ssem_i, rsem_i, to):
-        copy = pltpu.make_async_remote_copy(
-            src, dst, ssem.at[ssem_i], rsem.at[rsem_i], device_id=to, device_id_type=MESH
-        )
-        copy.start()
-        sent.append(copy)
+    def kind(total):
+        sends.append(total)
+        return len(sends) - 1
+
+    def push(src, dst, of, rsem_i, to):
+        pltpu.make_async_remote_copy(
+            src, dst, ssem.at[of], rsem.at[rsem_i], device_id=to, device_id_type=MESH
+        ).start()
 
     def arrive(dst, rsem_i):
         pltpu.make_async_remote_copy(
@@ -97,26 +98,24 @@
     place_of, length = (z, x), (NZ, NX)
     own, oth, rcv = (own_z, own_x), (oth_z, oth_x), (rcv_z, rcv_x)
     g_shard, g_pair = group(1), (group(8), group(4))
+    s_shard, s_pair = kind(shard.at[1]), (kind(rcv_z), kind(rcv_x))
 
     def push_pair(a):
-        for i, k in enumerate(orders[a] if RS else []):
+        for i, k in enumerate(orders[a]):
             dest = lax.rem(place_of[a] + k + length[a], length[a])
-            push(oth[a].at[dest], rcv[a].at[dest], g_pair[a] + i, g_pair[a] + i, at(dc=1))
+            push(oth[a].at[dest], rcv[a].at[dest], s_pair[a], g_pair[a] + i, at(dc=1))
 
     cot_loads[0].wait()
     partials(1 - c, oth_z, oth_x, (0, 1))
     loads[2].wait()
     shard[0] = jnp.concatenate([shard_in[...].astype(F32), jnp.zeros((4, D), F32)], axis=0).astype(BF16)
-    def rs(f, *args):
-        return f(*args) if RS else None
-
-    def ag(f, *args):
-        return f(*args) if AG else None
-
     qs = [c * 4 + lax.rem(x + k, 4) for k in range(4)] + [(1 - c) * 4 + lax.rem(x + k, 4) for k in range(4)]
     yls = [yl, lax.rem(yl + 3, 4), lax.rem(yl + 1, 4), lax.rem(yl + 2, 4)]
     low, high = pl.ds(0, 4), pl.ds(4, 4)
-    g_wz, g_wz_s, g_wy, g_wx, g_wc = group(8), group(7), group(4), group(16), group(16)
+    g_wz, g_wy, g_wx, g_wf, g_wc = group(1), group(3), group(8), group(4), group(4)
+    s_wz, s_wy, s_wx, s_wf, s_wc = [
+        kind(t) for t in (blocks.at[0, 0, pl.ds(0, 7)], blocks.at[0, pl.ds(0, 3)], blocks.at[pl.ds(0, 2)], blocks.at[0], blocks.at[pl.ds(0, 4)])
+    ]
 
     def make_unit():
         q = qs[0]
@@ -127,29 +126,22 @@
         unit[SHARD : 2 * SHARD, :] = jnp.where(first, others, mine)
         u = unit[...]
         blocks[q, yl, z] = jnp.concatenate([u[:, :128], u[:, 128:]], axis=0).astype(BF16)
-        for i, k in enumerate((4, 3, -3, 2, -2, 1, -1)):
-            push(blocks.at[q, yl, z], blocks.at[q, yl, z], g_wz_s + i, g_wz + z, at(dz=k))
+        for k in (4, 3, -3, 2, -2, 1, -1):
+            push(blocks.at[q, yl, z], blocks.at[q, yl, z], s_wz, g_wz, at(dz=k))
 
     def along_y():
         q = qs[0]
-        for k in range(1, 8):
-            zk = lax.rem(z + k, 8)
-            arrive(blocks.at[q, yl, zk], g_wz + zk)
-        push(blocks.at[q, yl], blocks.at[q, yl], g_wy, g_wy, at(dy=1))
-        push(blocks.at[q, yl], blocks.at[q, yl], g_wy + 1, g_wy + 1, at(dy=-1))
-        push(blocks.at[q, yl, low], blocks.at[q, yl, low], g_wy + 2, g_wy + 2, at(dy=2))
-        push(blocks.at[q, yl, high], blocks.at[q, yl, high], g_wy + 3, g_wy + 3, at(dy=-2))
+        arrive(blocks.at[q, yl, pl.ds(0, 7)], g_wz)
+        push(blocks.at[q, yl], blocks.at[q, yl], s_wy, g_wy, at(dy=1))
+        push(blocks.at[q, yl], blocks.at[q, yl], s_wy, g_wy + 1, at(dy=-1))
+        push(blocks.at[q, yl, low], blocks.at[q, yl, low], s_wy, g_wy + 2, at(dy=2))
+        push(blocks.at[q, yl, high], blocks.at[q, yl, high], s_wy, g_wy + 2, at(dy=-2))
 
     pl.semaphore_wait(barrier, len(peers))
-    if AG:
-        push(shard.at[0], shard.at[1], g_shard, g_shard, at(dc=1))
+    push(shard.at[0], shard.at[1], s_shard, g_shard, at(dc=1))
     push_pair(0)
     partials(1 - c, oth_z, oth_x, (2, 3))
     push_pair(1)
-    if AG:
-        make_unit()
-    cot_loads[1].wait()
-    partials(c, own_z, own_x, (0, 1, 2, 3))
 
     paired = set()
 
@@ -162,27 +154,27 @@
         return dest
 
     rings, height = (ring_z, ring_x), (48, 192)
-    g_ring = (group(32), group(16))
-
-    def slot(a, d, sub, t):
-        return ((d * 4) + sub) * (length[a] // 2) + t - 1
-
-    def ring_step(a, t):
-        for i in range(2 if t == 1 else 4):
+    g_ring = (group(28), group(12))
+    s_ring = (kind(ring_z), kind(ring_x))
+
+    def slot(a, d, i, t, far):
+        return 2 * d + i if t == 1 else 4 + 8 * (t - 2) + 4 * far + 2 * d + i
+
+    def ring_step(a, t, far):
+        for i in range(2):
             for d in range(2):
-                far = t == 1 or i >= 2
-                sub = (i % 2) + 2 * (d if far else 1 - d)
+                sub = i + 2 * (d if far else 1 - d)
                 dest = pair(a, (length[a] // 2 + 1 - t) * (1 if d == 0 else -1))
                 rows = pl.ds(height[a] * sub, height[a])
                 total = own[a][dest, rows, :].astype(F32) + rcv[a][dest, rows, :].astype(F32)
                 if t > 2 or (t == 2 and far):
-                    m = slot(a, d, sub, t - 1)
+                    m = slot(a, d, i, t - 1, far)
                     arrive(rings[a].at[m], g_ring[a] + m)
                     total = total + rings[a][m].astype(F32)
                 own[a][dest, rows, :] = total.astype(BF16)
-                m = slot(a, d, sub, t)
+                m = slot(a, d, i, t, far)
                 step = 1 if d == 0 else -1
-                push(own[a].at[dest, rows, :], rings[a].at[m], g_ring[a] + m, g_ring[a] + m,
+                push(own[a].at[dest, rows, :], rings[a].at[m], s_ring[a], g_ring[a] + m,
                      at(dz=step) if a == 0 else at(dx=step))
 
     def ring_end(a):
@@ -191,50 +183,48 @@
         for sub in range(4):
             rows = pl.ds(height[a] * sub, height[a])
             ends.append(own[a][dest, rows, :].astype(F32) + rcv[a][dest, rows, :].astype(F32))
-        for i in range(4):
-            for d in range(2):
-                sub = (i % 2) + 2 * (1 - d if i < 2 else d)
-                m = slot(a, d, sub, length[a] // 2)
-                arrive(rings[a].at[m], g_ring[a] + m)
-                ends[sub] = ends[sub] + rings[a][m].astype(F32)
+        for far in (False, True):
+            for i in range(2):
+                for d in range(2):
+                    sub = i + 2 * (d if far else 1 - d)
+                    m = slot(a, d, i, length[a] // 2, far)
+                    arrive(rings[a].at[m], g_ring[a] + m)
+                    ends[sub] = ends[sub] + rings[a][m].astype(F32)
         return ends
 
     def to_core(k, j):
         block = blocks.at[qs[k], yls[j]]
-        push(block, block, g_wc + 4 * k + j, g_wc + 4 * k + j, at(dc=1))
+        push(block, block, s_wc, g_wc + k, at(dc=1))
 
     def spread(j):
         if j in (1, 2):
             arrive(blocks.at[qs[0], yls[j]], g_wy + j - 1)
         if j == 3:
-            arrive(blocks.at[qs[0], yls[3], low], g_wy + 2)
-            arrive(blocks.at[qs[0], yls[3], high], g_wy + 3)
+            arrive(blocks.at[qs[0], yls[3]], g_wy + 2)
         block = blocks.at[qs[0], yls[j]]
-        push(block, block, g_wx + j, g_wx + j, at(dx=1))
-        push(block, block, g_wx + 4 + j, g_wx + 4 + j, at(dx=-1))
+        push(block, block, s_wx, g_wx + j, at(dx=1))
+        push(block, block, s_wx, g_wx + 4 + j, at(dx=-1))
         to_core(0, j)
 
     def forward(j):
         arrive(blocks.at[qs[3], yls[j]], g_wx + j)
         part = blocks.at[qs[3], yls[j], low]
-        push(part, part, g_wx + 8 + j, g_wx + 8 + j, at(dx=1))
+        push(part, part, s_wf, g_wf + j, at(dx=1))
         arrive(blocks.at[qs[1], yls[j]], g_wx + 4 + j)
         part = blocks.at[qs[1], yls[j], high]
-        push(part, part, g_wx + 12 + j, g_wx + 12 + j, at(dx=-1))
+        push(part, part, s_wf, g_wf + j, at(dx=-1))
         to_core(3, j)
         to_core(1, j)
 
     def last(j):
-        arrive(blocks.at[qs[2], yls[j], low], g_wx + 8 + j)
-        arrive(blocks.at[qs[2], yls[j], high], g_wx + 12 + j)
+        arrive(blocks.at[qs[2], yls[j]], g_wf + j)
         to_core(2, j)
 
-    stores = []
+    stores, done = [], []
 
     def multiply(i):
         if i >= 4:
-            for j in range(4):
-                arrive(blocks.at[qs[i], yls[j]], g_wc + 4 * (i - 4) + j)
+            arrive(blocks.at[qs[i]], g_wc + i - 4)
         qi = qs[i]
         for zi in range(8):
             for h in range(2):
@@ -247,31 +237,32 @@
             at_k = pl.ds(pl.multiple_of(qi * 256 + 128 * k, 128), 128)
             out[:, at_k] = (wgt[...] * p).astype(BF16)
             term = cot[:, at_k].astype(F32) * p
-            gp_acc[...] = term if not stores and k == 0 else gp_acc[...] + term
+            gp_acc[...] = term if not done and k == 0 else gp_acc[...] + term
         back = lax.dot_general(scaled[:, cols], full[i], (((1,), (1,)), ((), ())), preferred_element_type=F32)
-        gh_acc[...] = back if not stores else gh_acc[...] + back
-        copy = pltpu.make_async_copy(out.at[:, cols], out_h.at[:, cols], local.at[5 + i])
-        copy.start()
-        stores.append(copy)
+        gh_acc[...] = back if not done else gh_acc[...] + back
+        pltpu.make_async_copy(out.at[:, cols], out_h.at[:, cols], local.at[5]).start()
+        done.append(i)
 
     far_first = (4, 3, -3, 2, -2, 1, -1)
-    g_z, g_z_s, g_yz, g_yz_s, g_yx, g_yx_s = group(8), group(7), group(8), group(7), group(8), group(7)
-    g_x, g_x_s, g_core = group(4), group(3), group(1)
+    g_z, g_yz, g_yx, g_x, g_core = [group(1) for _ in range(5)]
+    seven = pl.ds(0, 7)
+    s_z, s_yz, s_yx = kind(recv_z.at[seven]), kind(recv_yz.at[seven]), kind(recv_yx.at[seven])
+    s_x, s_core = kind(recv_x.at[pl.ds(0, 3)]), kind(core_r)
     none = jnp.zeros((8, 128), F32)
 
     def across_z():
         ends = ring_end(1)
         for k in range(8):
             send_z[k] = ends[k // 2][96 * (k % 2) : 96 * (k % 2) + 96].astype(BF16)
-        for i, k in enumerate(far_first):
+        for k in far_first:
             to = lax.rem(z + k + 8, 8)
-            push(send_z.at[to], recv_z.at[z], g_z_s + i, g_z + z, at(dz=k))
+            push(send_z.at[to], recv_z.at[z], s_z, g_z, at(dz=k))
         recv_z[z] = send_z[z]
 
-    def across_y(send, recv, base, base_s):
-        for i, k in enumerate(far_first):
+    def across_y(send, recv, base, of):
+        for k in far_first:
             to = lax.rem(yl + k + 4, 4)
-            push(send.at[to], recv.at[y], base_s + i, base + y, at(dy=k))
+            push(send.at[to], recv.at[y], of, base, at(dy=k))
         recv[y] = send[yl]
 
     def across_y_z():
@@ -281,36 +272,34 @@
             low_cols, high_cols = ends[k // 2][rows], ends[2 + k // 2][rows]
             parts = [low_cols[:, :128], low_cols[:, 128:], high_cols[:, :128], high_cols[:, 128:]]
             send_yz[k] = jnp.concatenate(parts, axis=0).astype(BF16)
-        across_y(send_yz, recv_yz, g_yz, g_yz_s)
-
-    def gathered(recv, base, mine, n):
-        for k in range(1, n):
-            at_k = lax.rem(mine + k, n)
-            arrive(recv.at[at_k], base + at_k)
+        across_y(send_yz, recv_yz, g_yz, s_yz)
+
+    def gathered(recv, base, n):
+        arrive(recv.at[pl.ds(0, n - 1)], base)
         total = recv[0].astype(F32)
         for k in range(1, n):
             total = total + recv[k].astype(F32)
         return total
 
     def across_y_x():
-        total = gathered(recv_z, g_z, z, 8)
+        total = gathered(recv_z, g_z, 8)
         for k in range(4):
             send_yx[k] = jnp.concatenate([total[24 * k : 24 * k + 24], none], axis=0).astype(BF16)
-        across_y(send_yx, recv_yx, g_yx, g_yx_s)
+        across_y(send_yx, recv_yx, g_yx, s_yx)
 
     def exchange_x():
-        total_z = gathered(recv_yz, g_yz, y, 8)
-        total_x = gathered(recv_yx, g_yx, y, 8)
+        total_z = gathered(recv_yz, g_yz, 8)
+        total_x = gathered(recv_yx, g_yx, 8)
         recv_x[x] = jnp.concatenate([total_z, total_x], axis=0).astype(BF16)
-        for i, k in enumerate((2, 1, 3)):
-            push(recv_x.at[x], recv_x.at[x], g_x_s + i, g_x + x, at(dx=k))
+        for k in (2, 1, 3):
+            push(recv_x.at[x], recv_x.at[x], s_x, g_x, at(dx=k))
 
     def exchange_core():
-        total = gathered(recv_x, g_x, x, 4)
+        total = gathered(recv_x, g_x, 4)
         core_s[pl.ds(0, 96), :] = total[:96]
         for k in range(4):
             core_s[pl.ds(96 + 24 * k, 24), :] = recv_x[k].astype(F32)[96:120]
-        push(core_s, core_r, g_core, g_core, at(dc=1))
+        push(core_s, core_r, s_core, g_core, at(dc=1))
 
     def finish_sum():
         arrive(core_r, g_core)
@@ -319,55 +308,77 @@
             for k in range(8):
                 part = f[24 * k : 24 * k + 24]
                 gw[:, pl.ds(h * (D // 2) + 128 * k, 128)] = jnp.where(first, part[:SHARD], part[SHARD:])
-        copy = pltpu.make_async_copy(gw, gw_h, local.at[13])
+        copy = pltpu.make_async_copy(gw, gw_h, local.at[7])
         copy.start()
         stores.append(copy)
 
-    rs(ring_step, 0, 1)
-    rs(ring_step, 1, 1)
-    rs(ring_step, 1, 2)
-    rs(ring_step, 0, 2)
-    ag(along_y)
-    ag(spread, 0)
-    rs(ring_step, 0, 3)
-    rs(ring_step, 0, 4)
-    rs(across_z)
-    ag(spread, 1)
-    ag(spread, 2)
-    ag(forward, 0)
-    rs(across_y_z)
-    ag(spread, 3)
-    rs(across_y_x)
-    ag(multiply, 0)
-    ag(forward, 1)
-    ag(forward, 2)
-    ag(multiply, 4)
-    rs(exchange_x)
-    ag(forward, 3)
-    for j in range(3):
-        ag(last, j)
-    ag(multiply, 1)
-    ag(multiply, 3)
-    rs(exchange_core)
-    ag(last, 3)
-    ag(multiply, 5)
-    rs(finish_sum)
-    ag(multiply, 7)
-    ag(multiply, 2)
-    ag(multiply, 6)
+    cot_loads[1].wait()
+    partials(c, own_z, own_x, (0, 1))
+    ring_step(0, 1, True)
+    partials(c, own_z, own_x, (2, 3))
+    ring_step(1, 1, True)
+    ring_step(0, 2, False)
+    make_unit()
+    ring_step(0, 2, True)
+    ring_step(1, 2, False)
+    ring_step(1, 2, True)
+    ring_step(0, 3, False)
+    ring_step(0, 3, True)
+    along_y()
+    spread(0)
+    ring_step(0, 4, False)
+    ring_step(0, 4, True)
+    across_z()
+    spread(1)
+    spread(2)
+    forward(0)
+    across_y_z()
+    spread(3)
+    multiply(0)
+    across_y_x()
+    forward(1)
+    forward(2)
+    multiply(4)
+    forward(3)
+    multiply(1)
+    multiply(3)
+    exchange_x()
+    last(0)
+    last(1)
+    last(2)
+    last(3)
+    multiply(5)
+    multiply(7)
+    exchange_core()
+    multiply(2)
+    multiply(6)
+    finish_sum()
     gh[...] = gh_acc[...].astype(BF16)
-    copy = pltpu.make_async_copy(gh, gh_h, local.at[13])
+    copy = pltpu.make_async_copy(gh, gh_h, local.at[6])
     copy.start()
     stores.append(copy)
     gp[...] = (live_row * jnp.sum(gp_acc[...].T, axis=0, keepdims=True)).reshape(ROWS)
-    copy = pltpu.make_async_copy(gp, gp_h, local.at[14])
+    copy = pltpu.make_async_copy(gp, gp_h, local.at[8])
     copy.start()
     stores.append(copy)
 
     for copy in stores:
         copy.wait()
-    for copy in sent:
-        copy.wait_send()
+    pltpu.make_async_copy(out, out_h, local.at[5]).wait()
+    assert len(sends) == KINDS and used[0] == SEMS
+    for of, total in enumerate(sends):
+        pltpu.make_async_remote_copy(
+            total, total, ssem.at[of], rsem.at[0], device_id=at(dc=1), device_id_type=MESH
+        ).wait_send()
+
+
+def hand_over(*refs):
+    n = (len(refs) - 1) // 2
+    copies = [pltpu.make_async_copy(refs[i], refs[n + i], refs[-1].at[i]) for i in range(n)]
+    for copy in copies:
+        copy.start()
+    for copy in copies:
+        copy.wait()
 
 
 def pin(a):
@@ -402,8 +413,8 @@
             vmem((4, FF, 128), BF16),
             vmem((8, 192, 256), BF16),
             vmem((4, FF, 128), BF16),
-            vmem((32, 48, 256), BF16),
-            vmem((16, 192, 128), BF16),
+            vmem((28, 48, 256), BF16),
+            vmem((12, 192, 128), BF16),
             vmem((SHARD, D), BF16),
             vmem((2, 16, D), BF16),
             vmem((2 * SHARD, 256), F32),
@@ -424,15 +435,24 @@
             vmem((192, 128), F32),
             vmem((192, 128), F32),
             vmem((SHARD, D), F32),
-            pltpu.SemaphoreType.DMA((16,)),
-            pltpu.SemaphoreType.DMA((SEMS,)),
+            pltpu.SemaphoreType.DMA((9,)),
+            pltpu.SemaphoreType.DMA((KINDS,)),
             pltpu.SemaphoreType.DMA((SEMS,)),
         ],
         compiler_params=pltpu.CompilerParams(
             collective_id=0, has_side_effects=True, vmem_limit_bytes=40 * 2**20
         ),
     )(pin(hidden), pin(prob), counts, pin(down_weight), pin(cotangent))
-    return output, grad_hidden, grad_prob, grad_weight
+    results = (output, grad_hidden, grad_prob, grad_weight)
+    return pl.pallas_call(
+        hand_over,
+        name="hand_over",
+        out_shape=tuple(jax.ShapeDtypeStruct(a.shape, a.dtype) for a in results),
+        in_specs=[pl.BlockSpec(memory_space=pltpu.VMEM)] * 4,
+        out_specs=(free,) * 4,
+        scratch_shapes=[pltpu.SemaphoreType.DMA((4,))],
+        compiler_params=pltpu.CompilerParams(vmem_limit_bytes=8 * 2**20),
+    )(*results)
 
 
 def solution(mesh):

time: 58.4 us -> 49.9 us (0.85)
  Pallas kernels: 53.7 us -> 48.5 us
  local copies, waits for them, and re-layouts: 3.19 us -> 0 us
    pallas_call x1, Pallas kernels: 53.7 us -> 47.1 us  [body(): pl.pallas_call(kernel, name='expert_down', out_shape=(jax.ShapeDtypeStruc...]
    unnamed x4 -> x0, local copies, waits for them, and re-layouts: 3.19 us -> none
    pallas_call x0 -> x1, Pallas kernels: none -> 1.41 us  [body(): pl.pallas_call(hand_over, name='hand_over', out_shape=tuple((jax.ShapeDty...]
where the time goes in v3:
time: 49.9 us; the launch traced here: 49.8 us
  Pallas kernels  48.5 us (97%)
  between operations  1.29 us (3%)
    pallas_call x1, Pallas kernels, body(): pl.pallas_call(kernel, name='expert_down', out_shape=(jax.ShapeDtypeStruc...  47.1 us
    pallas_call x1, Pallas kernels, body(): pl.pallas_call(hand_over, name='hand_over', out_shape=tuple((jax.ShapeDty...  1.41 us

profile of v3, /device:TPU:1, one launch (start us, length us, event | category | flops | bytes accessed | tf_op | source)
XLA Modules:
  0.0 49.8 jit_solution(17800647482912728817)
XLA Ops:
  1.3 47.1 %expert_down.1 = (bf16[384,2048]{1,0:T(8,128)(2,1)S(1)}, bf16[384,768]{1,0:T(8,128)(2,1)S(1)}, f32[384]{0:T(512)S(1)}, f32[12,2048]{1,0:T(8,128)S(1)}) custom-call(bf16[384,768]{1,0:T(8,128)(2,1)} %hidden_h.1, f32[384]{0:T(512)} %prob_h.1, s32[1]{0:T(128)S(6)} %copy.9.counts_s, bf16[12,2048]{1,0:T(8,128)(2,1)} %weight_h.1, bf16[384,2048]{1,0:T(8,128)(2,1)} %cot_h.1), custom_call_target="tpu_custom_call" | custom-call | tf_op jit(solution)/shard_map/expert_down/pallas_call | solution.py:392
  48.4 1.4 %hand_over.1 = (bf16[384,2048]{1,0:T(8,128)(2,1)}, bf16[384,768]{1,0:T(8,128)(2,1)}, f32[384]{0:T(512)}, f32[12,2048]{1,0:T(8,128)}) custom-call(bf16[384,2048]{1,0:T(8,128)(2,1)S(1)} %get-tuple-element.8.refs_0_, bf16[384,768]{1,0:T(8,128)(2,1)S(1)} %get-tuple-element.9.refs_1_, f32[384]{0:T(512)S(1)} %get-tuple-element.10.refs_2_, ...), custom_call_target="tpu_custom_call" | custom-call | tf_op jit(solution)/shard_map/hand_over/pallas_call | solution.py:447

commit v4 on v3

--- a/solution.py
+++ b/solution.py
@@ -9,7 +9,7 @@
 F32, BF16 = jnp.float32, jnp.bfloat16
 NX, NY, NZ, LO = 4, 8, 8, 4
 ROWS, FF, D, SHARD = 384, 768, 2048, 12
-SEMS, KINDS = 78, 15
+SEMS, KINDS = 57, 14
 
 
 def device(x, y, z, c):
@@ -19,8 +19,8 @@
 
 def kernel(
     hidden_h, prob_h, counts_s, weight_h, cot_h, out_h, gh_h, gp_h, gw_h,
-    hid, hid_t, cot, scaled, prob, wgt, own_z, own_x, oth_z, oth_x, rcv_z, rcv_x, ring_z, ring_x, shard_in, shard, unit,
-    blocks, full, out, gh_acc, gh, gp_acc, gp, send_z, recv_z, send_yz, recv_yz, send_yx, recv_yx, recv_x, core_s, core_r, gw,
+    hid, hid_t, cot, scaled, prob, wgt, own_z, own_x, oth_z, oth_x, rcv_z, rcv_x, ring_z, ring_x, shard_in, z_mine, z_other, unit, order_z,
+    blocks, full, out, gh_acc, gh, gp_acc, gp, send_z, recv_z, send_yz, recv_yz, send_yx, recv_yx, mix, send_x, recv_x, gw,
     local, ssem, rsem,
 ):
     r, s = lax.axis_index("rep"), lax.axis_index("shard")
@@ -31,12 +31,6 @@
 
     def at(dx=0, dy=0, dz=0, dc=0):
         return device(x + dx + NX, y + dy + NY, z + dz + NZ, c + dc)
-
-    barrier = pltpu.get_barrier_semaphore()
-    peers = [at(dc=1)] + [at(dx=k) for k in (1, 2, 3)]
-    peers += [at(dy=k) for k in range(1, 8)] + [at(dz=k) for k in range(1, 8)]
-    for peer in peers:
-        pl.semaphore_signal(barrier, inc=1, device_id=peer, device_id_type=MESH)
 
     loads = [
         pltpu.make_async_copy(a, b, local.at[i])
@@ -51,6 +45,13 @@
         load.start()
         cot_loads.append(load)
 
+    barrier = pltpu.get_barrier_semaphore()
+    peers = [at(dc=1)] + [at(dx=k) for k in (1, 2, 3)]
+    peers += [at(dx=k, dc=1) for k in (1, 2, 3)]
+    peers += [at(dy=k) for k in range(1, 8)] + [at(dz=k) for k in range(1, 8)]
+    for peer in peers:
+        pl.semaphore_signal(barrier, inc=1, device_id=peer, device_id_type=MESH)
+
     used, sends = [0], []
 
     def group(n):
@@ -74,7 +75,7 @@
 
     loads[0].wait()
     place = lax.broadcasted_iota(jnp.int32, (1, ROWS), 1)
-    live_row = (place < counts_s[0]).astype(F32)
+    live_row = (place < counts_s[...].reshape(1, 1)).astype(F32)
     row = prob[...].reshape(1, ROWS) * live_row
     wgt[...] = jnp.broadcast_to(row, (128, ROWS)).T
     loads[1].wait()
@@ -83,11 +84,11 @@
     def partials(half, keep_z, keep_x, ns):
         for n in ns:
             start = half * (D // 2) + 256 * n
-            for k in range(2):
-                at_k = pl.ds(pl.multiple_of(start + 128 * k, 128), 128)
-                scaled[:, at_k] = (wgt[...] * cot[:, at_k].astype(F32)).astype(BF16)
             cols = pl.ds(pl.multiple_of(start, 256), 256)
-            part = jnp.dot(hid_t[...], scaled[:, cols], preferred_element_type=F32)
+            two = jnp.concatenate([wgt[...], wgt[...]], axis=1)
+            piece = (two * cot[:, cols].astype(F32)).astype(BF16)
+            scaled[(4 if keep_z is own_z else 0) + n] = piece
+            part = jnp.dot(hid_t[...], piece, preferred_element_type=F32)
             if n < 2:
                 keep_z[:, pl.ds(96 * n, 96), :] = part.astype(BF16).reshape(8, 96, 256)
             else:
@@ -98,7 +99,7 @@
     place_of, length = (z, x), (NZ, NX)
     own, oth, rcv = (own_z, own_x), (oth_z, oth_x), (rcv_z, rcv_x)
     g_shard, g_pair = group(1), (group(8), group(4))
-    s_shard, s_pair = kind(shard.at[1]), (kind(rcv_z), kind(rcv_x))
+    s_shard, s_pair = kind(z_other), (kind(rcv_z), kind(rcv_x))
 
     def push_pair(a):
         for i, k in enumerate(orders[a]):
@@ -108,37 +109,46 @@
     cot_loads[0].wait()
     partials(1 - c, oth_z, oth_x, (0, 1))
     loads[2].wait()
-    shard[0] = jnp.concatenate([shard_in[...].astype(F32), jnp.zeros((4, D), F32)], axis=0).astype(BF16)
+    for h in range(2):
+        for b in range(2):
+            cols = pl.ds(pl.multiple_of(h * (D // 2) + x * 256 + 128 * b, 128), 128)
+            unit[pl.ds(24 * h + SHARD * b, SHARD), :] = shard_in[:, cols].astype(F32)
+    z_mine[z] = unit[...].astype(BF16)
     qs = [c * 4 + lax.rem(x + k, 4) for k in range(4)] + [(1 - c) * 4 + lax.rem(x + k, 4) for k in range(4)]
     yls = [yl, lax.rem(yl + 3, 4), lax.rem(yl + 1, 4), lax.rem(yl + 2, 4)]
     low, high = pl.ds(0, 4), pl.ds(4, 4)
     g_wz, g_wy, g_wx, g_wf, g_wc = group(1), group(3), group(8), group(4), group(4)
     s_wz, s_wy, s_wx, s_wf, s_wc = [
-        kind(t) for t in (blocks.at[0, 0, pl.ds(0, 7)], blocks.at[0, pl.ds(0, 3)], blocks.at[pl.ds(0, 2)], blocks.at[0], blocks.at[pl.ds(0, 4)])
+        kind(t) for t in (z_mine.at[pl.ds(0, 7)], blocks.at[0, pl.ds(0, 3)], blocks.at[pl.ds(0, 2)], blocks.at[0], blocks.at[pl.ds(0, 4)])
     ]
 
-    def make_unit():
-        q = qs[0]
-        arrive(shard.at[1], g_shard)
-        cols = pl.ds(pl.multiple_of(q * 256, 256), 256)
-        mine, others = shard[0, :, cols].astype(F32)[:SHARD], shard[1, :, cols].astype(F32)[:SHARD]
-        unit[0:SHARD, :] = jnp.where(first, mine, others)
-        unit[SHARD : 2 * SHARD, :] = jnp.where(first, others, mine)
-        u = unit[...]
-        blocks[q, yl, z] = jnp.concatenate([u[:, :128], u[:, 128:]], axis=0).astype(BF16)
+    def send_unit():
         for k in (4, 3, -3, 2, -2, 1, -1):
-            push(blocks.at[q, yl, z], blocks.at[q, yl, z], s_wz, g_wz, at(dz=k))
+            push(z_mine.at[z], z_mine.at[z], s_wz, g_wz, at(dz=k))
+
+    def swap():
+        arrive(z_mine.at[pl.ds(0, 7)], g_wz)
+        push(z_mine, z_other, s_shard, g_shard, at(dc=1))
 
     def along_y():
         q = qs[0]
-        arrive(blocks.at[q, yl, pl.ds(0, 7)], g_wz)
+        arrive(z_other, g_shard)
+        mine, others = z_mine[...].astype(F32), z_other[...].astype(F32)
+        mine = jnp.where(first, mine[:, :24], mine[:, 24:])
+        others = jnp.where(first, others[:, :24], others[:, 24:])
+        even, odd = jnp.where(first, mine, others), jnp.where(first, others, mine)
+        for b in range(2):
+            from_b = slice(SHARD * b, SHARD * b + SHARD)
+            order_z[:, pl.ds(24 * b, SHARD), :] = even[:, from_b]
+            order_z[:, pl.ds(24 * b + SHARD, SHARD), :] = odd[:, from_b]
+        blocks[q, yl] = order_z[...].astype(BF16)
         push(blocks.at[q, yl], blocks.at[q, yl], s_wy, g_wy, at(dy=1))
         push(blocks.at[q, yl], blocks.at[q, yl], s_wy, g_wy + 1, at(dy=-1))
         push(blocks.at[q, yl, low], blocks.at[q, yl, low], s_wy, g_wy + 2, at(dy=2))
         push(blocks.at[q, yl, high], blocks.at[q, yl, high], s_wy, g_wy + 2, at(dy=-2))
 
     pl.semaphore_wait(barrier, len(peers))
-    push(shard.at[0], shard.at[1], s_shard, g_shard, at(dc=1))
+    send_unit()
     push_pair(0)
     partials(1 - c, oth_z, oth_x, (2, 3))
     push_pair(1)
@@ -153,17 +163,17 @@
             arrive(rcv[a].at[dest], g_pair[a] + orders[a].index(k))
         return dest
 
-    rings, height = (ring_z, ring_x), (48, 192)
-    g_ring = (group(28), group(12))
+    rings, height = (ring_z, ring_x), (96, 384)
+    g_ring = (group(14), group(6))
     s_ring = (kind(ring_z), kind(ring_x))
 
     def slot(a, d, i, t, far):
-        return 2 * d + i if t == 1 else 4 + 8 * (t - 2) + 4 * far + 2 * d + i
+        return d if t == 1 else 2 + 4 * (t - 2) + 2 * far + d
 
     def ring_step(a, t, far):
-        for i in range(2):
+        for i in range(1):
             for d in range(2):
-                sub = i + 2 * (d if far else 1 - d)
+                sub = d if far else 1 - d
                 dest = pair(a, (length[a] // 2 + 1 - t) * (1 if d == 0 else -1))
                 rows = pl.ds(height[a] * sub, height[a])
                 total = own[a][dest, rows, :].astype(F32) + rcv[a][dest, rows, :].astype(F32)
@@ -180,13 +190,13 @@
     def ring_end(a):
         dest = pair(a, 0)
         ends = []
-        for sub in range(4):
+        for sub in range(2):
             rows = pl.ds(height[a] * sub, height[a])
             ends.append(own[a][dest, rows, :].astype(F32) + rcv[a][dest, rows, :].astype(F32))
         for far in (False, True):
-            for i in range(2):
+            for i in range(1):
                 for d in range(2):
-                    sub = i + 2 * (d if far else 1 - d)
+                    sub = d if far else 1 - d
                     m = slot(a, d, i, length[a] // 2, far)
                     arrive(rings[a].at[m], g_ring[a] + m)
                     ends[sub] = ends[sub] + rings[a][m].astype(F32)
@@ -238,22 +248,22 @@
             out[:, at_k] = (wgt[...] * p).astype(BF16)
             term = cot[:, at_k].astype(F32) * p
             gp_acc[...] = term if not done and k == 0 else gp_acc[...] + term
-        back = lax.dot_general(scaled[:, cols], full[i], (((1,), (1,)), ((), ())), preferred_element_type=F32)
+        back = lax.dot_general(scaled[(4 if i < 4 else 0) + lax.rem(qi, 4)], full[i], (((1,), (1,)), ((), ())), preferred_element_type=F32)
         gh_acc[...] = back if not done else gh_acc[...] + back
         pltpu.make_async_copy(out.at[:, cols], out_h.at[:, cols], local.at[5]).start()
         done.append(i)
 
     far_first = (4, 3, -3, 2, -2, 1, -1)
-    g_z, g_yz, g_yx, g_x, g_core = [group(1) for _ in range(5)]
+    g_z, g_yz, g_yx, g_x = [group(1) for _ in range(4)]
     seven = pl.ds(0, 7)
     s_z, s_yz, s_yx = kind(recv_z.at[seven]), kind(recv_yz.at[seven]), kind(recv_yx.at[seven])
-    s_x, s_core = kind(recv_x.at[pl.ds(0, 3)]), kind(core_r)
+    s_x = kind(recv_x.at[seven])
     none = jnp.zeros((8, 128), F32)
 
     def across_z():
         ends = ring_end(1)
         for k in range(8):
-            send_z[k] = ends[k // 2][96 * (k % 2) : 96 * (k % 2) + 96].astype(BF16)
+            send_z[k] = ends[k // 4][96 * (k % 4) : 96 * (k % 4) + 96].astype(BF16)
         for k in far_first:
             to = lax.rem(z + k + 8, 8)
             push(send_z.at[to], recv_z.at[z], s_z, g_z, at(dz=k))
@@ -268,8 +278,8 @@
     def across_y_z():
         ends = ring_end(0)
         for k in range(4):
-            rows = slice(24 * (k % 2), 24 * (k % 2) + 24)
-            low_cols, high_cols = ends[k // 2][rows], ends[2 + k // 2][rows]
+            rows = slice(24 * k, 24 * k + 24)
+            low_cols, high_cols = ends[0][rows], ends[1][rows]
             parts = [low_cols[:, :128], low_cols[:, 128:], high_cols[:, :128], high_cols[:, 128:]]
             send_yz[k] = jnp.concatenate(parts, axis=0).astype(BF16)
         across_y(send_yz, recv_yz, g_yz, s_yz)
@@ -290,25 +300,39 @@
     def exchange_x():
         total_z = gathered(recv_yz, g_yz, 8)
         total_x = gathered(recv_yx, g_yx, 8)
-        recv_x[x] = jnp.concatenate([total_z, total_x], axis=0).astype(BF16)
+        for d in range(2):
+            for k in range(4):
+                mix[d, pl.ds(SHARD * k, SHARD), :] = total_z[24 * k + SHARD * d : 24 * k + SHARD * d + SHARD]
+            mix[d, pl.ds(4 * SHARD, SHARD), :] = total_x[SHARD * d : SHARD * d + SHARD]
+            mix[d, pl.ds(5 * SHARD, 4), :] = jnp.zeros((4, 128), F32)
+        send_x[...] = mix[...].astype(BF16)
+        here = recv_x.at[c * 4 + x]
         for k in (2, 1, 3):
-            push(recv_x.at[x], recv_x.at[x], s_x, g_x, at(dx=k))
-
-    def exchange_core():
-        total = gathered(recv_x, g_x, 4)
-        core_s[pl.ds(0, 96), :] = total[:96]
-        for k in range(4):
-            core_s[pl.ds(96 + 24 * k, 24), :] = recv_x[k].astype(F32)[96:120]
-        push(core_s, core_r, s_core, g_core, at(dc=1))
+            push(send_x.at[1 - c], here, s_x, g_x, at(dx=k, dc=1))
+        for k in (2, 1, 3):
+            push(send_x.at[c], here, s_x, g_x, at(dx=k))
+        push(send_x.at[1 - c], here, s_x, g_x, at(dc=1))
+        recv_x[c * 4 + x] = send_x[c]
 
     def finish_sum():
-        arrive(core_r, g_core)
+        arrive(recv_x.at[seven], g_x)
         for h in range(2):
-            f = jnp.where(first, core_s[...], core_r[...]) if h == 0 else jnp.where(first, core_r[...], core_s[...])
-            for k in range(8):
-                part = f[24 * k : 24 * k + 24]
-                gw[:, pl.ds(h * (D // 2) + 128 * k, 128)] = jnp.where(first, part[:SHARD], part[SHARD:])
+            parts = [recv_x[4 * h + k].astype(F32) for k in range(4)]
+            total = parts[0] + parts[1] + parts[2] + parts[3]
+            for k in range(4):
+                gw[:, pl.ds(h * (D // 2) + 128 * k, 128)] = total[SHARD * k : SHARD * k + SHARD]
+                gw[:, pl.ds(h * (D // 2) + 512 + 128 * k, 128)] = parts[k][4 * SHARD : 5 * SHARD]
         copy = pltpu.make_async_copy(gw, gw_h, local.at[7])
+        copy.start()
+        stores.append(copy)
+
+    def finish_rest():
+        gh[...] = gh_acc[...].astype(BF16)
+        copy = pltpu.make_async_copy(gh, gh_h, local.at[6])
+        copy.start()
+        stores.append(copy)
+        gp[...] = (live_row * jnp.sum(gp_acc[...].T, axis=0, keepdims=True)).reshape(ROWS)
+        copy = pltpu.make_async_copy(gp, gp_h, local.at[8])
         copy.start()
         stores.append(copy)
 
@@ -318,10 +342,10 @@
     partials(c, own_z, own_x, (2, 3))
     ring_step(1, 1, True)
     ring_step(0, 2, False)
-    make_unit()
     ring_step(0, 2, True)
     ring_step(1, 2, False)
     ring_step(1, 2, True)
+    swap()
     ring_step(0, 3, False)
     ring_step(0, 3, True)
     along_y()
@@ -332,36 +356,27 @@
     spread(1)
     spread(2)
     forward(0)
+    spread(3)
     across_y_z()
-    spread(3)
     multiply(0)
+    forward(1)
     across_y_x()
-    forward(1)
     forward(2)
     multiply(4)
     forward(3)
     multiply(1)
+    exchange_x()
     multiply(3)
-    exchange_x()
     last(0)
     last(1)
     last(2)
+    multiply(5)
     last(3)
-    multiply(5)
     multiply(7)
-    exchange_core()
     multiply(2)
     multiply(6)
+    finish_rest()
     finish_sum()
-    gh[...] = gh_acc[...].astype(BF16)
-    copy = pltpu.make_async_copy(gh, gh_h, local.at[6])
-    copy.start()
-    stores.append(copy)
-    gp[...] = (live_row * jnp.sum(gp_acc[...].T, axis=0, keepdims=True)).reshape(ROWS)
-    copy = pltpu.make_async_copy(gp, gp_h, local.at[8])
-    copy.start()
-    stores.append(copy)
-
     for copy in stores:
         copy.wait()
     pltpu.make_async_copy(out, out_h, local.at[5]).wait()
@@ -398,13 +413,13 @@
             jax.ShapeDtypeStruct((ROWS,), F32),
             jax.ShapeDtypeStruct((SHARD, D), F32),
         ),
-        in_specs=[hbm, hbm, pl.BlockSpec(memory_space=pltpu.SMEM), hbm, hbm],
+        in_specs=[hbm, hbm, pl.BlockSpec(memory_space=pltpu.VMEM), hbm, hbm],
         out_specs=(free, free, free, free),
         scratch_shapes=[
             vmem((ROWS, FF), BF16),
             vmem((FF, ROWS), BF16),
             vmem((ROWS, D), BF16),
-            vmem((ROWS, D), BF16),
+            vmem((8, ROWS, 256), BF16),
             vmem((ROWS,), F32),
             vmem((ROWS, 128), F32),
             vmem((8, 192, 256), BF16),
@@ -413,11 +428,13 @@
             vmem((4, FF, 128), BF16),
             vmem((8, 192, 256), BF16),
             vmem((4, FF, 128), BF16),
-            vmem((28, 48, 256), BF16),
-            vmem((12, 192, 128), BF16),
+            vmem((14, 96, 256), BF16),
+            vmem((6, 384, 128), BF16),
             vmem((SHARD, D), BF16),
-            vmem((2, 16, D), BF16),
-            vmem((2 * SHARD, 256), F32),
+            vmem((8, 48, 128), BF16),
+            vmem((8, 48, 128), BF16),
+            vmem((48, 128), F32),
+            vmem((8, 48, 128), F32),
             vmem((8, 4, 8, 48, 128), BF16),
             vmem((8, FF, 256), BF16),
             vmem((ROWS, D), BF16),
@@ -431,9 +448,9 @@
             vmem((8, 96, 128), BF16),
             vmem((4, 32, 128), BF16),
             vmem((8, 32, 128), BF16),
-            vmem((4, 128, 128), BF16),
-            vmem((192, 128), F32),
-            vmem((192, 128), F32),
+            vmem((2, 64, 128), F32),
+            vmem((2, 64, 128), BF16),
+            vmem((8, 64, 128), BF16),
             vmem((SHARD, D), F32),
             pltpu.SemaphoreType.DMA((9,)),
             pltpu.SemaphoreType.DMA((KINDS,)),

time: 49.9 us -> 48.2 us (0.966)
  Pallas kernels: 48.5 us -> 46.7 us
    pallas_call x1, Pallas kernels: 47.1 us -> 45.3 us  [body(): pl.pallas_call(kernel, name='expert_down', out_shape=(jax.ShapeDtypeStruc...]
where the time goes in v4:
time: 48.2 us; the launch traced here: 48 us
  Pallas kernels  46.7 us (97%)
  between operations  1.29 us (3%)
    pallas_call x1, Pallas kernels, body(): pl.pallas_call(kernel, name='expert_down', out_shape=(jax.ShapeDtypeStruc...  45.3 us
    pallas_call x1, Pallas kernels, body(): pl.pallas_call(hand_over, name='hand_over', out_shape=tuple((jax.ShapeDty...  1.41 us

profile of v4, /device:TPU:1, one launch (start us, length us, event | category | flops | bytes accessed | tf_op | source)
XLA Modules:
  0.0 48.0 jit_solution(1320619416968134920)
XLA Ops:
  1.3 45.3 %expert_down.1 = (bf16[384,2048]{1,0:T(8,128)(2,1)S(1)}, bf16[384,768]{1,0:T(8,128)(2,1)S(1)}, f32[384]{0:T(512)S(1)}, f32[12,2048]{1,0:T(8,128)S(1)}) custom-call(bf16[384,768]{1,0:T(8,128)(2,1)} %hidden_h.1, f32[384]{0:T(512)} %prob_h.1, s32[1]{0:T(128)S(6)} %copy.9.counts_s, bf16[12,2048]{1,0:T(8,128)(2,1)} %weight_h.1, bf16[384,2048]{1,0:T(8,128)(2,1)} %cot_h.1), custom_call_target="tpu_custom_call" | custom-call | tf_op jit(solution)/shard_map/expert_down/pallas_call | solution.py:407
  46.6 1.4 %hand_over.1 = (bf16[384,2048]{1,0:T(8,128)(2,1)}, bf16[384,768]{1,0:T(8,128)(2,1)}, f32[384]{0:T(512)}, f32[12,2048]{1,0:T(8,128)}) custom-call(bf16[384,2048]{1,0:T(8,128)(2,1)S(1)} %get-tuple-element.8.refs_0_, bf16[384,768]{1,0:T(8,128)(2,1)S(1)} %get-tuple-element.9.refs_1_, f32[384]{0:T(512)S(1)} %get-tuple-element.10.refs_2_, ...), custom_call_target="tpu_custom_call" | custom-call | tf_op jit(solution)/shard_map/hand_over/pallas_call | solution.py:464

commit v5 on v4

--- a/solution.py
+++ b/solution.py
@@ -249,7 +249,10 @@
             term = cot[:, at_k].astype(F32) * p
             gp_acc[...] = term if not done and k == 0 else gp_acc[...] + term
         back = lax.dot_general(scaled[(4 if i < 4 else 0) + lax.rem(qi, 4)], full[i], (((1,), (1,)), ((), ())), preferred_element_type=F32)
-        gh_acc[...] = back if not done else gh_acc[...] + back
+        if len(done) == 7:
+            gh[...] = (gh_acc[...] + back).astype(BF16)
+        else:
+            gh_acc[...] = back if not done else gh_acc[...] + back
         pltpu.make_async_copy(out.at[:, cols], out_h.at[:, cols], local.at[5]).start()
         done.append(i)
 
@@ -327,7 +330,6 @@
         stores.append(copy)
 
     def finish_rest():
-        gh[...] = gh_acc[...].astype(BF16)
         copy = pltpu.make_async_copy(gh, gh_h, local.at[6])
         copy.start()
         stores.append(copy)
@@ -360,8 +362,8 @@
     across_y_z()
     multiply(0)
     forward(1)
+    forward(2)
     across_y_x()
-    forward(2)
     multiply(4)
     forward(3)
     multiply(1)

time: 48.2 us -> 48.1 us (level)
  no operation moved by 1% of the time
where the time goes in v5:
time: 48.1 us; the launch traced here: 47.9 us
  Pallas kernels  46.7 us (97%)
  between operations  1.29 us (3%)
    pallas_call x1, Pallas kernels, body(): pl.pallas_call(kernel, name='expert_down', out_shape=(jax.ShapeDtypeStruc...  45.2 us
    pallas_call x1, Pallas kernels, body(): pl.pallas_call(hand_over, name='hand_over', out_shape=tuple((jax.ShapeDty...  1.41 us

profile of v5, /device:TPU:1, one launch (start us, length us, event | category | flops | bytes accessed | tf_op | source)
XLA Modules:
  0.0 47.9 jit_solution(14026192455137254700)
XLA Ops:
  1.3 45.2 %expert_down.1 = (bf16[384,2048]{1,0:T(8,128)(2,1)S(1)}, bf16[384,768]{1,0:T(8,128)(2,1)S(1)}, f32[384]{0:T(512)S(1)}, f32[12,2048]{1,0:T(8,128)S(1)}) custom-call(bf16[384,768]{1,0:T(8,128)(2,1)} %hidden_h.1, f32[384]{0:T(512)} %prob_h.1, s32[1]{0:T(128)S(6)} %copy.9.counts_s, bf16[12,2048]{1,0:T(8,128)(2,1)} %weight_h.1, bf16[384,2048]{1,0:T(8,128)(2,1)} %cot_h.1), custom_call_target="tpu_custom_call" | custom-call | tf_op jit(solution)/shard_map/expert_down/pallas_call | solution.py:409
  46.5 1.4 %hand_over.1 = (bf16[384,2048]{1,0:T(8,128)(2,1)}, bf16[384,768]{1,0:T(8,128)(2,1)}, f32[384]{0:T(512)}, f32[12,2048]{1,0:T(8,128)}) custom-call(bf16[384,2048]{1,0:T(8,128)(2,1)S(1)} %get-tuple-element.8.refs_0_, bf16[384,768]{1,0:T(8,128)(2,1)S(1)} %get-tuple-element.9.refs_1_, f32[384]{0:T(512)S(1)} %get-tuple-element.10.refs_2_, ...), custom_call_target="tpu_custom_call" | custom-call | tf_op jit(solution)/shard_map/hand_over/pallas_call | solution.py:466
